TPU v7x, 256 devices: a whole 4x4x8 slice. The times are simulated.
256 devices in a mesh: seq: 32 (over y, z_hi, core), head: 8 (over x, z_lo).
Axes of the slice: x: 4, y: 4, z: 8 (z_hi: 4, z_lo: 2; z = z_hi * 2 + z_lo), core: 2. Of those that a mesh axis runs over, the one named last changes fastest.
Arguments:
- prompt_qkv: bfloat16 [3, 2048, 4096], P(None, 'seq', 'head'), may hold values from -16 to 16
- prompt_grad: bfloat16 [2048, 4096], P('seq', 'head'), may hold values from -6 to 6
- comp_qkv: bfloat16 [3, 32, 256, 4096], P(None, 'seq', 'head'), may hold values from -16 to 16
- comp_grad: bfloat16 [32, 256, 4096], P('seq', 'head'), may hold values from -6 to 6
- lengths: int32 [32], P('seq'), may hold values from 64 to 256, as said below
- keep_mask: int32 [32, 256], P('seq'), may hold values 0 or 1
Outputs:
- prompt_out: bfloat16 [2048, 4096], P('seq', 'head')
- comp_out: bfloat16 [32, 256, 4096], P('seq', 'head')
- prompt_dqkv: bfloat16 [3, 2048, 4096], P(None, 'seq', 'head')
- comp_dqkv: bfloat16 [3, 32, 256, 4096], P(None, 'seq', 'head')
Inputs may be any that keep to these rules, and one draw needn't show every extreme that they name: `lengths`: every length lies in 64..256, and at least one completion has length 256.
All inputs are finite; a program needn't handle non-finite values. No bound on the sum of `keep_mask` on one device may be relied on, other than what follows from the above.
Results may differ from a plain program's by a relative error of at most 0.033.
Values may be sent and summed in bfloat16 or wider, within the bound.
A program may use at most 128 MiB of HBM per device.

v0:
```python
import math

import jax
import jax.numpy as jnp
from jax import lax
from jax.sharding import PartitionSpec as P

HEAD_DIM = 128


def far_scores(query, keys, factor):
    return jnp.einsum("clhe,phe->chlp", query, keys, preferred_element_type=jnp.float32) * factor


def row_delta(cot, out):
    summed = jnp.sum(cot.astype(jnp.float32) * out.astype(jnp.float32), axis=3)
    return jnp.transpose(summed, (0, 2, 1))[..., None]


def local(prompt_qkv, prompt_grad, comp_qkv, comp_grad, lengths, keep_mask):
    local_width = prompt_grad.shape[1]
    local_heads = local_width // HEAD_DIM
    factor = 1.0 / math.sqrt(HEAD_DIM)
    comps_here = comp_qkv.shape[1]
    length = keep_mask.shape[1]
    prompt_here = prompt_grad.shape[0]
    bf16 = jnp.bfloat16
    arrived, arrived_grad = (
        lax.all_to_all(comp_qkv, "head", split_axis=3, concat_axis=2, tiled=True),
        lax.all_to_all(comp_grad[None], "head", split_axis=3, concat_axis=2, tiled=True),
    )
    split = (comps_here, length, local_heads, HEAD_DIM)
    comp_query = arrived[0].reshape(split)
    comp_keys = arrived[1].reshape(split)
    comp_values = arrived[2].reshape(split)
    position = lax.iota(jnp.int32, length)
    valid = (position[None, :] < lengths[:, None]) & (keep_mask == 1)
    comp_cot = arrived_grad[0].reshape(split) * valid[:, :, None, None].astype(bf16)
    gathered = lax.all_gather(prompt_qkv[1:], "seq", axis=1, tiled=True)
    prompt_keys = gathered[0].reshape(-1, local_heads, HEAD_DIM)
    prompt_values = gathered[1].reshape(-1, local_heads, HEAD_DIM)
    prompt_query = prompt_qkv[0].reshape(1, prompt_here, local_heads, HEAD_DIM)
    prompt_cot = prompt_grad.reshape(1, prompt_here, local_heads, HEAD_DIM)
    score_self = far_scores(prompt_query, prompt_keys, factor)
    top_self = jnp.max(score_self, axis=3, keepdims=True)
    lse_self = top_self + jnp.log(jnp.sum(jnp.exp(score_self - top_self), axis=3, keepdims=True))
    prob_self = jnp.exp(score_self - lse_self)
    weight_self = prob_self.astype(bf16)
    out_self = jnp.einsum(
        "chlp,phe->clhe", weight_self, prompt_values, preferred_element_type=jnp.float32
    ).astype(bf16)
    score_far = far_scores(comp_query, prompt_keys, factor)
    score_near = (
        jnp.einsum("clhe,cjhe->chlj", comp_query, comp_keys, preferred_element_type=jnp.float32)
        * factor
    )
    score_near = jnp.where(valid[:, None, None, :], score_near, -jnp.inf)
    top = jnp.maximum(
        jnp.max(score_far, axis=3, keepdims=True), jnp.max(score_near, axis=3, keepdims=True)
    )
    total = jnp.sum(jnp.exp(score_far - top), axis=3, keepdims=True) + jnp.sum(
        jnp.exp(score_near - top), axis=3, keepdims=True
    )
    lse = top + jnp.log(total)
    prob_far = jnp.exp(score_far - lse)
    prob_near = jnp.exp(score_near - lse)
    weight_far = prob_far.astype(bf16)
    weight_near = prob_near.astype(bf16)
    comp_out = (
        jnp.einsum("chlp,phe->clhe", weight_far, prompt_values, preferred_element_type=jnp.float32)
        + jnp.einsum(
            "chlj,cjhe->clhe", weight_near, comp_values, preferred_element_type=jnp.float32
        )
    ).astype(bf16)
    comp_flat = comp_out.reshape(comps_here, length, local_width)
    delta_self = row_delta(prompt_cot, out_self)
    grad_self = jnp.einsum(
        "clhe,phe->chlp", prompt_cot, prompt_values, preferred_element_type=jnp.float32
    )
    ds_self = (prob_self * (grad_self - delta_self) * factor).astype(bf16)
    dq_self = jnp.einsum("chlp,phe->clhe", ds_self, prompt_keys, preferred_element_type=jnp.float32)
    delta = row_delta(comp_cot, comp_out)
    grad_far = jnp.einsum(
        "clhe,phe->chlp", comp_cot, prompt_values, preferred_element_type=jnp.float32
    )
    grad_near = jnp.einsum(
        "clhe,cjhe->chlj", comp_cot, comp_values, preferred_element_type=jnp.float32
    )
    ds_far = (prob_far * (grad_far - delta) * factor).astype(bf16)
    ds_near = (prob_near * (grad_near - delta) * factor).astype(bf16)
    dq_comp = jnp.einsum(
        "chlp,phe->clhe", ds_far, prompt_keys, preferred_element_type=jnp.float32
    ) + jnp.einsum("chlj,cjhe->clhe", ds_near, comp_keys, preferred_element_type=jnp.float32)
    dk_comp = jnp.einsum("chlj,clhe->cjhe", ds_near, comp_query, preferred_element_type=jnp.float32)
    dv_comp = jnp.einsum(
        "chlj,clhe->cjhe", weight_near, comp_cot, preferred_element_type=jnp.float32
    )
    count = prompt_keys.shape[0]
    dkeys = jnp.einsum(
        "chlp,clhe->phe", ds_far, comp_query, preferred_element_type=jnp.float32
    ) + jnp.einsum("chlp,clhe->phe", ds_self, prompt_query, preferred_element_type=jnp.float32)
    dvalues = jnp.einsum(
        "chlp,clhe->phe", weight_far, comp_cot, preferred_element_type=jnp.float32
    ) + jnp.einsum("chlp,clhe->phe", weight_self, prompt_cot, preferred_element_type=jnp.float32)
    summed = lax.psum_scatter(
        jnp.concatenate([dkeys.reshape(count, -1), dvalues.reshape(count, -1)], axis=1).astype(
            jnp.bfloat16
        ),
        "seq",
        scatter_dimension=0,
        tiled=True,
    ).astype(jnp.float32)
    prompt_dqkv = jnp.stack(
        [
            dq_self.reshape(prompt_here, local_width),
            summed[:, :local_width],
            summed[:, local_width:],
        ]
    ).astype(bf16)
    prompt_out = out_self.reshape(prompt_here, local_width)
    comp_grads = (
        jnp.stack([dq_comp, dk_comp, dv_comp])
        .astype(bf16)
        .reshape(3, comps_here, length, local_width)
    )
    back_both, back_grads = (
        lax.all_to_all(comp_flat[None], "head", split_axis=2, concat_axis=3, tiled=True),
        lax.all_to_all(comp_grads, "head", split_axis=2, concat_axis=3, tiled=True),
    )
    back_out = back_both[0]
    return (prompt_out, back_out, prompt_dqkv, back_grads)


def solution(mesh):
    in_specs = (
        P(None, "seq", "head"),
        P("seq", "head"),
        P(None, "seq", "head", None),
        P("seq", "head", None),
        P("seq"),
        P("seq", None),
    )
    out_specs = (
        P("seq", "head"),
        P("seq", "head", None),
        P(None, "seq", "head"),
        P(None, "seq", "head", None),
    )
    return jax.shard_map(local, mesh=mesh, in_specs=in_specs, out_specs=out_specs, check_vma=False)
```

profile of v0, /device:TPU:1, one launch (start us, length us, event | category | flops | bytes accessed | tf_op | source)
XLA Modules:
  0.0 273.8 jit_solution(1467731986478717927)
XLA Ops:
  9.0 4.5 %copy.266 = bf16[1,1,32,4096]{2,1,0,3:T(2,128)(2,1)S(1)} copy(bf16[1,1,32,4096]{3,2,1,0:T(8,128)(2,1)} %bitcast.288) | data formatting | bytes 524288 | tf_op jit(solution)/shard_map/broadcast_in_dim | solution.py:30
  14.0 22.4 %reduce.12 = bf16[4096,32]{1,0:T(8,128)(2,1)S(1)} reduce(bf16[4096,1,1,32]{3,2,1,0:T(2,128)(2,1)S(1)} %bitcast.273, bf16[]{:T(256)} %broadcast.83), dimensions={1,2}, to_apply=%bitcast.225.reduce_sub_computation | reduce | bytes 524290
  36.5 1.7 reshape.332
  38.2 6.2 %all-to-all-start.2 = ((bf16[8,2,8192]{2,1,0:T(2,128)(2,1)}), bf16[8,2,8192]{2,1,0:T(2,128)(2,1)S(1)}, u32[]{:S(2)}, u32[]{:S(2)}) async-start(bf16[8,2,8192]{2,1,0:T(2,128)(2,1)} %reshape.332), calls=%async_computation.2 | async-start | bytes 524288 | tf_op jit(solution)/shard_map/all_to_all | solution.py:30
  44.4 6.0 %copy.247 = bf16[3,1,32,4096]{2,0,1,3:T(4,128)(2,1)} copy(bf16[3,1,32,4096]{3,2,1,0:T(8,128)(2,1)} %param.8) | data formatting | bytes 1572864 | tf_op args[2]
  50.4 7.3 %reshape.328 = bf16[8,2,24576]{2,1,0:T(2,128)(2,1)} reshape(bf16[4096,1,3,32]{3,2,1,0:T(4,128)(2,1)} %bitcast.271) | data formatting | bytes 1572864
  57.7 5.1 %all-to-all-start = ((bf16[8,2,24576]{2,1,0:T(2,128)(2,1)}), bf16[8,2,24576]{2,1,0:T(2,128)(2,1)S(1)}, u32[]{:S(2)}, u32[]{:S(2)}) async-start(bf16[8,2,24576]{2,1,0:T(2,128)(2,1)} %reshape.328), calls=%async_computation | async-start | bytes 1572864 | tf_op jit(solution)/shard_map/all_to_all | solution.py:29
  64.5 1.3 reshape.333
  65.8 2.1 copy.267
  70.4 11.3 %all-to-all-done = bf16[8,2,24576]{2,1,0:T(2,128)(2,1)S(1)} async-done(((bf16[8,2,24576]{2,1,0:T(2,128)(2,1)}), bf16[8,2,24576]{2,1,0:T(2,128)(2,1)S(1)}, u32[]{:S(2)}, u32[]{:S(2)}) %all-to-all-start) | async-done | bytes 786464 | tf_op jit(solution)/shard_map/all_to_all | solution.py:29
  81.7 4.9 %reshape.329 = bf16[4096,1,3,32]{3,2,1,0:T(4,128)(2,1)} reshape(bf16[8,2,24576]{2,1,0:T(2,128)(2,1)S(1)} %all-to-all-done) | data formatting | bytes 1572864
  86.6 4.2 %copy.314 = bf16[3,1,32,8,512]{4,3,2,0,1:T(8,128)(2,1)S(1)} copy(bf16[3,1,32,8,512]{2,0,4,3,1:T(4,128)(2,1)} %bitcast.270) | data formatting | bytes 1572864 | tf_op jit(solution)/shard_map/all_to_all | solution.py:29
  92.8 10.0 %fusion.64 = (bf16[1,2048,512]{2,0,1:T(2,128)(2,1)}, bf16[1,2048,512]{2,0,1:T(2,128)(2,1)}) fusion(bf16[2,2048,512]{2,0,1:T(2,128)(2,1)} %all-gather.2.cloned.1.call-done), kind=kLoop, calls=%fused_computation.84 | loop fusion | bytes 8388608 | tf_op jit(solution)/shard_map/slice | solution.py:40
  102.8 9.0 %copy.318 = bf16[1,2048,512]{1,2,0:T(8,128)(2,1)S(1)} copy(bf16[1,2048,512]{2,0,1:T(2,128)(2,1)} %get-tuple-element.20) | data formatting | bytes 4194304
  111.8 1.3 bitcast_reduce_fusion
  113.3 1.4 fusion.5
  114.7 1.7 copy-done
  116.4 10.6 %copy.317 = bf16[1,2048,512]{1,2,0:T(8,128)(2,1)} copy(bf16[1,2048,512]{2,0,1:T(2,128)(2,1)} %get-tuple-element.21) | data formatting | bytes 4194304
  127.0 1.3 convolution_bitcast_fusion.2
  128.3 6.4 %multiply_reduce_fusion = (f32[256,4]{0,1:T(4,128)S(1)}, bf16[1,256,4,128]{1,3,2,0:T(8,128)(2,1)}) fusion(bf16[1,256,4,128]{1,3,2,0:T(8,128)(2,1)} %copy.273, bf16[256]{0:T(256)(128)(2,1)} %copy-done.12, f32[1,256,4,128]{1,3,2,0:T(8,128)S(1)} %convolution_bitcast_fusion.2, bf16[2048,4,128]{0,2,1:T(8,128)(2,1)} %bitcast.266, f32[4,2048,256]{2,1,0:T(8,128)} %copy-done, ...), kind=kOutput, calls=%fused_computation.58 | convolution fusion | flops 544078848 | bytes 11543040 | tf_op jit(solution)/shard_map/chlp,phe->clhe/dot_general | solution.py:70
  135.4 3.0 %fusion.3 = bf16[1,4,256,2048]{2,3,1,0:T(8,128)(2,1)S(1)} fusion(f32[4,2048,256]{2,1,0:T(8,128)S(1)} %copy-done.1, bf16[2048,4,128]{0,2,1:T(8,128)(2,1)S(1)} %bitcast.267, f32[4,256]{1,0:T(4,128)S(1)} %bitcast.292, f32[4,256]{1,0:T(4,128)S(1)} %log_add_fusion, bf16[256,4,128]{2,1,0:T(4,128)(2,1)S(1)} %copy-done.7), kind=kOutput, calls=%fused_computation.4 | convolution fusion | flops 549453824 | bytes 14950400 | tf_op jit(solution)/shard_map/clhe,phe->chlp/dot_general | solution.py:83
  139.4 2.7 fusion.45
  142.1 1.6 fusion.54
  144.6 1.0 copy-done.4
  146.3 2.8 %add_convert_fusion = bf16[4,2048,128]{1,2,0:T(8,128)(2,1)} fusion(f32[4,2048,128]{1,2,0:T(8,128)S(1)} %fusion.59, bf16[256,4,128]{0,2,1:T(8,128)(2,1)S(1)} %copy.275, bf16[1,4,256,2048]{2,3,1,0:T(8,128)(2,1)S(1)} %fusion.3), kind=kOutput, calls=%fused_computation.20 | convolution fusion | flops 538968064 | bytes 10747904 | tf_op jit(solution)/shard_map/chlp,clhe->phe/dot_general | solution.py:99
  149.1 3.9 %copy.280 = bf16[2048,512]{1,0:T(8,128)(2,1)} copy(bf16[2048,512]{0,1:T(8,128)(2,1)} %bitcast.275) | data formatting | bytes 4194304 | tf_op jit(solution)/shard_map/reshape | solution.py:106
  153.0 7.8 %fusion.9 = bf16[2048,4,128]{0,2,1:T(8,128)(2,1)} fusion(f32[4,2048,128]{1,2,0:T(8,128)} %fusion.45, bf16[256,4,128]{0,2,1:T(8,128)(2,1)} %copy.277, f32[4,2048,256]{2,1,0:T(8,128)} %copy-done, f32[4,256]{1,0:T(4,128)S(1)} %log_add_fusion), kind=kOutput, calls=%fused_computation.15 | convolution fusion | flops 545259520 | bytes 14946304 | tf_op jit(solution)/shard_map/chlp,clhe->phe/dot_general | solution.py:102
  160.9 3.9 %copy.281 = bf16[2048,512]{1,0:T(8,128)(2,1)} copy(bf16[2048,512]{0,1:T(8,128)(2,1)} %bitcast.274) | data formatting | bytes 4194304 | tf_op jit(solution)/shard_map/reshape | solution.py:106
  164.8 4.7 %pad_maximum_fusion = bf16[2048,1024]{1,0:T(8,128)(2,1)} fusion(bf16[2048,512]{1,0:T(8,128)(2,1)} %copy.281, bf16[2048,512]{1,0:T(8,128)(2,1)} %copy.280), kind=kLoop, calls=%fused_computation.13 | loop fusion | flops 8388608 | bytes 8388608 | tf_op jit(solution)/shard_map/concatenate | solution.py:106
  169.5 2.0 copy.259
  171.5 3.9 %reduce.13 = bf16[256,512]{1,0:T(8,128)(2,1)} reduce(bf16[256,1,1,512]{3,2,1,0:T(2,128)(2,1)} %bitcast.279, bf16[]{:T(256)} %broadcast.83), dimensions={1,2}, to_apply=%bitcast.223.reduce_sub_computation | reduce | bytes 524290
  175.3 1.9 reshape.330
  177.2 4.3 %all-to-all-start.1 = ((bf16[8,2,8192]{2,1,0:T(2,128)(2,1)}), bf16[8,2,8192]{2,1,0:T(2,128)(2,1)}, u32[]{:S(2)}, u32[]{:S(2)}) async-start(bf16[8,2,8192]{2,1,0:T(2,128)(2,1)} %reshape.330), calls=%async_computation.1 | async-start | bytes 524288 | tf_op jit(solution)/shard_map/all_to_all | solution.py:127
  181.5 1.4 fusion.27
  182.9 1.2 convolution_bitcast_fusion.1
  184.1 3.7 %fusion.36 = bf16[1,256,4,128]{1,3,2,0:T(8,128)(2,1)} fusion(f32[1,256,4,128]{1,3,2,0:T(8,128)S(1)} %convolution_bitcast_fusion.1, bf16[2048,4,128]{0,2,1:T(8,128)(2,1)S(1)} %bitcast.264, bf16[1,4,256,2048]{2,3,1,0:T(8,128)(2,1)} %copy-done.3), kind=kOutput, calls=%fused_computation.46 | convolution fusion | flops 537133056 | bytes 7077888 | tf_op jit(solution)/shard_map/chlp,phe->clhe/dot_general | solution.py:91
  187.9 1.0 convolution_convert_fusion.1
  188.9 2.0 copy.292
  190.9 2.0 copy.293
  192.9 1.3 convolution_convert_fusion
  194.2 1.1 copy.294
  195.3 4.2 %pad_maximum_fusion.1 = bf16[3,1,256,512]{3,0,1,2:T(4,128)(2,1)} fusion(bf16[1,1,256,512]{3,0,1,2:T(2,128)(2,1)} %copy.294, bf16[1,1,256,512]{3,0,1,2:T(2,128)(2,1)} %copy.293, bf16[1,1,256,512]{3,0,1,2:T(2,128)(2,1)} %copy.292), kind=kLoop, calls=%fused_computation.54 | loop fusion | flops 2359296 | bytes 1572864 | tf_op jit(solution)/shard_map/stack | solution.py:122
  199.5 4.8 %all-to-all-start.3 = ((bf16[3,1,256,512]{3,0,1,2:T(4,128)(2,1)}), bf16[3,1,256,512]{3,0,1,2:T(4,128)(2,1)}, u32[]{:S(2)}, u32[]{:S(2)}) async-start(bf16[3,1,256,512]{3,0,1,2:T(4,128)(2,1)} %pad_maximum_fusion.1), calls=%async_computation.4 | async-start | bytes 2097152 | tf_op jit(solution)/shard_map/all_to_all | solution.py:128
  205.9 1.2 reshape.331
  208.1 10.3 %all-to-all-done.3 = bf16[3,1,256,512]{3,0,1,2:T(4,128)(2,1)} async-done(((bf16[3,1,256,512]{3,0,1,2:T(4,128)(2,1)}), bf16[3,1,256,512]{3,0,1,2:T(4,128)(2,1)}, u32[]{:S(2)}, u32[]{:S(2)}) %all-to-all-start.3) | async-done | bytes 786464 | tf_op jit(solution)/shard_map/all_to_all | solution.py:128
  218.4 1.7 copy.295
  220.1 1.0 copy.321
  221.0 44.4 %reduce-scatter.2.cloned.1.call-done = bf16[64,1024]{1,0:T(8,128)(2,1)} async-done(((bf16[2048,1024]{1,0:T(8,128)(2,1)}), bf16[64,1024]{1,0:T(8,128)(2,1)}) %reduce-scatter.2.cloned.1.call-update) | async-done | bytes 131088 | tf_op jit(solution)/shard_map/reduce_scatter | solution.py:105
  (76 shorter events, 15.3 us)
Async XLA Ops:
  7.2 85.7 %all-gather.2.cloned.1.call-start = ((), (), s32[]{:S(2)}) async-start(), calls=%async_computation.5 | async-start | bytes 4325376 | tf_op jit(solution)/shard_map/all_gather | solution.py:39
  38.2 19.6 %all-to-all-start.2 = ((bf16[8,2,8192]{2,1,0:T(2,128)(2,1)}), bf16[8,2,8192]{2,1,0:T(2,128)(2,1)S(1)}, u32[]{:S(2)}, u32[]{:S(2)}) async-start(bf16[8,2,8192]{2,1,0:T(2,128)(2,1)} %reshape.332), calls=%async_computation.2 | async-start | bytes 524288 | tf_op jit(solution)/shard_map/all_to_all | solution.py:30
  50.4 13.3 %copy-start.13 = (s32[1,256]{1,0:T(1,128)S(1)}, s32[1,256]{1,0:T(1,128)}, u32[]{:S(2)}) copy-start(s32[1,256]{1,0:T(1,128)} %param.11) | copy-start | bytes 3076
  50.4 13.3 %slice-start = ((bf16[3,64,512]{2,1,0:T(8,128)(2,1)}), bf16[1,64,512]{2,1,0:T(8,128)(2,1)S(1)}, s32[]{:S(2)}) async-start(bf16[3,64,512]{2,1,0:T(8,128)(2,1)} %param.6), calls=%async_computation.7 | async-start | bytes 131072 | tf_op jit(solution)/shard_map/slice | solution.py:42
  50.4 13.4 %copy-start.9 = (bf16[64,512]{1,0:T(8,128)(2,1)S(1)}, bf16[64,512]{1,0:T(8,128)(2,1)}, u32[]{:S(2)}) copy-start(bf16[64,512]{1,0:T(8,128)(2,1)} %param.7) | copy-start | bytes 196612
  57.7 23.9 %all-to-all-start = ((bf16[8,2,24576]{2,1,0:T(2,128)(2,1)}), bf16[8,2,24576]{2,1,0:T(2,128)(2,1)S(1)}, u32[]{:S(2)}, u32[]{:S(2)}) async-start(bf16[8,2,24576]{2,1,0:T(2,128)(2,1)} %reshape.328), calls=%async_computation | async-start | bytes 1572864 | tf_op jit(solution)/shard_map/all_to_all | solution.py:29
  62.8 202.6 %reduce-scatter.2.cloned.1.call-start = ((), (), s32[]{:S(2)}) async-start(), calls=%async_computation.6 | async-start | bytes 4325376 | tf_op jit(solution)/shard_map/reduce_scatter | solution.py:105
  63.7 6.6 %copy-start.12 = (bf16[256]{0:T(256)(128)(2,1)}, bf16[256]{0:T(256)(128)(2,1)S(1)}, u32[]{:S(2)}) copy-start(bf16[256]{0:T(256)(128)(2,1)S(1)} %convert_element_type.99) | copy-start | bytes 1540
  69.5 21.3 %copy-start.6 = (bf16[256,4,128]{2,1,0:T(4,128)(2,1)}, bf16[256,4,128]{2,1,0:T(4,128)(2,1)S(1)}, u32[]{:S(2)}) copy-start(bf16[256,4,128]{2,1,0:T(4,128)(2,1)S(1)} %broadcast_multiply_fusion) | copy-start | bytes 786436
  91.6 11.3 %copy-start.8 = (bf16[256,4,128]{0,2,1:T(8,128)(2,1)}, bf16[256,4,128]{0,2,1:T(8,128)(2,1)S(1)}, u32[]{:S(2)}) copy-start(bf16[256,4,128]{0,2,1:T(8,128)(2,1)S(1)} %copy.287) | copy-start | bytes 786436
  113.1 3.2 %copy-start = (f32[4,2048,256]{2,1,0:T(8,128)}, f32[4,2048,256]{2,1,0:T(8,128)S(1)}, u32[]{:S(2)}) copy-start(f32[4,2048,256]{2,1,0:T(8,128)S(1)} %get-tuple-element.30) | copy-start | bytes 25165828
  128.2 6.5 %copy-start.1 = (f32[4,2048,256]{2,1,0:T(8,128)S(1)}, f32[4,2048,256]{2,1,0:T(8,128)}, u32[]{:S(2)}) copy-start(f32[4,2048,256]{2,1,0:T(8,128)} %copy-done) | copy-start | bytes 25165828
  128.3 7.1 %copy-start.2 = (bf16[1,2048,512]{1,2,0:T(8,128)(2,1)S(1)}, bf16[1,2048,512]{1,2,0:T(8,128)(2,1)}, u32[]{:S(2)}) copy-start(bf16[1,2048,512]{1,2,0:T(8,128)(2,1)} %copy.317) | copy-start | bytes 6291460
  128.3 7.1 %copy-start.7 = (bf16[256,4,128]{2,1,0:T(4,128)(2,1)S(1)}, bf16[256,4,128]{2,1,0:T(4,128)(2,1)}, u32[]{:S(2)}) copy-start(bf16[256,4,128]{2,1,0:T(4,128)(2,1)} %copy-done.6) | copy-start | bytes 786436
  138.4 7.9 %copy-start.3 = (bf16[1,4,256,2048]{2,3,1,0:T(8,128)(2,1)}, bf16[1,4,256,2048]{2,3,1,0:T(8,128)(2,1)S(1)}, u32[]{:S(2)}) copy-start(bf16[1,4,256,2048]{2,3,1,0:T(8,128)(2,1)S(1)} %fusion.3) | copy-start | bytes 12582916
  139.0 3.2 %copy-start.10 = (f32[1,64,4,128]{3,2,1,0:T(4,128)S(1)}, f32[1,64,4,128]{3,2,1,0:T(4,128)}, u32[]{:S(2)}) copy-start(f32[1,64,4,128]{3,2,1,0:T(4,128)} %reshape.326) | copy-start | bytes 393220
  144.6 1.0 copy-start.4
  177.2 22.3 %all-to-all-start.1 = ((bf16[8,2,8192]{2,1,0:T(2,128)(2,1)}), bf16[8,2,8192]{2,1,0:T(2,128)(2,1)}, u32[]{:S(2)}, u32[]{:S(2)}) async-start(bf16[8,2,8192]{2,1,0:T(2,128)(2,1)} %reshape.330), calls=%async_computation.1 | async-start | bytes 524288 | tf_op jit(solution)/shard_map/all_to_all | solution.py:127
  194.2 10.1 %copy-start.5 = (bf16[4,64,2048]{2,1,0:T(8,128)(2,1)S(1)}, bf16[4,64,2048]{2,1,0:T(8,128)(2,1)}, u32[]{:S(2)}) copy-start(bf16[4,64,2048]{2,1,0:T(8,128)(2,1)} %copy-done.4) | copy-start | bytes 3145732
  195.3 9.9 %copy-start.11 = (bf16[1,64,4,128]{3,1,2,0:T(8,128)(2,1)S(1)}, bf16[1,64,4,128]{3,1,2,0:T(8,128)(2,1)}, u32[]{:S(2)}) copy-start(bf16[1,64,4,128]{3,1,2,0:T(8,128)(2,1)} %get-tuple-element.34) | copy-start | bytes 196612
  199.5 18.8 %all-to-all-start.3 = ((bf16[3,1,256,512]{3,0,1,2:T(4,128)(2,1)}), bf16[3,1,256,512]{3,0,1,2:T(4,128)(2,1)}, u32[]{:S(2)}, u32[]{:S(2)}) async-start(bf16[3,1,256,512]{3,0,1,2:T(4,128)(2,1)} %pad_maximum_fusion.1), calls=%async_computation.4 | async-start | bytes 2097152 | tf_op jit(solution)/shard_map/all_to_all | solution.py:128
Sparse Core Ops, SparseCore 0:
  10.6 65.9 all-gather.1
  169.6 95.7 reduce-scatter.1
where the time goes:
time: 277 us; the launch traced here: 274 us
  local copies, waits for them, and re-layouts  94.8 us (34%)
  waiting for transfers between devices  66 us (24%)
  matrix products  38.9 us (14%)
  other arithmetic  38.3 us (14%)
  starting transfers between devices  20.6 us (7%)
  between operations  15.1 us (5%)
    unnamed x42, local copies, waits for them, and re-layouts  49.4 us
    reduce_scatter x1, waiting for transfers between devices, local(): lax.psum_scatter(jnp.concatenate([dkeys.reshape(count, -1), dvalues.resha...  44.4 us
    unnamed x2, other arithmetic  26.3 us
    all_to_all x1, waiting for transfers between devices, local(): lax.all_to_all(comp_qkv, 'head', split_axis=3, concat_axis=2, tiled=True)  11.3 us
    all_to_all x1, waiting for transfers between devices, local(): lax.all_to_all(comp_grads, 'head', split_axis=2, concat_axis=3, tiled=True)  10.3 us
    slice x1, local copies, waits for them, and re-layouts, local(): prompt_keys = gathered[0].reshape(-1, local_heads, HEAD_DIM)  9.98 us
    dot_general x1, matrix products, local(): jnp.einsum('chlp,clhe->phe', weight_far, comp_cot, preferred_element_type...  7.81 us
    dot_general x1, matrix products, local(): jnp.einsum('chlp,phe->clhe', weight_far, prompt_values, preferred_element...  6.43 us
  transfers between devices with their start and end apart: 6, of which 3 were waited for; matrix products, arithmetic and copies ran while one was open for 34% of the time, Pallas kernels for 0%

commit v1 on v0

v1 whole, which is shorter than its diff:
```python
import math

import jax
import jax.numpy as jnp
from jax import lax
from jax.experimental import pallas as pl
from jax.experimental.pallas import tpu as pltpu
from jax.sharding import PartitionSpec as P

MESH = pl.DeviceIdType.MESH
BF16 = jnp.bfloat16
F32 = jnp.float32

HEAD_DIM = 128
FACTOR = 1.0 / math.sqrt(HEAD_DIM)
EXP2_FACTOR = FACTOR * math.log2(math.e)
MASKED = -1e30

SLOTS = 256
COMP_ROWS = 2 * SLOTS
OWN = 64
BLOCK = 2 * OWN
ROWS = COMP_ROWS + BLOCK
WIDTH = 256
PROMPT = 2048
CHUNK = 512
HALF = CHUNK // 2
STEP = 256
TOKENS = 32
PEERS = 16


def dot_nt(a, b):
    return lax.dot_general(a, b, (((1,), (1,)), ((), ())), preferred_element_type=F32)


def dot_nn(a, b):
    return lax.dot_general(a, b, (((1,), (0,)), ((), ())), preferred_element_type=F32)


def dot_tn(a, b):
    return lax.dot_general(a, b, (((0,), (0,)), ((), ())), preferred_element_type=F32)


def fold_rows(value, op):
    return op(value.reshape(value.shape[0] // 8, 8, value.shape[1]), axis=0)


def await_bytes(ref, sem):
    pltpu.make_async_copy(ref, ref, sem).wait()


def remote(src, dst, send_sem, recv_sem, device):
    copy = pltpu.make_async_remote_copy(
        src_ref=src,
        dst_ref=dst,
        send_sem=send_sem,
        recv_sem=recv_sem,
        device_id=device,
        device_id_type=MESH,
    )
    copy.start()


def kernel(
    pqkv, pgrad, cqkv, cgrad, lengths, mask,
    pout, cout, pdqkv, cdqkv,
    kv, x, v01, e, eb, en, enb, ot, dqt, gp, dl, dp, y_buf, ra, rb, rc, rd, za, zb, zc, zd,
    local_sem, pair_send, pair_recv, swap_send, swap_recv, ag_send, ag_recv,
    rs_send, rs_recv, back_send, back_recv, last_send, last_recv,
):
    seq = lax.axis_index("seq")
    head = lax.axis_index("head")
    y = seq // 8
    z = (seq // 2) % 4
    core = seq % 2
    other = 1 - core

    def at(yy, zz, cc):
        return ((yy * 4 + zz) * 2 + cc, head)

    partner = at(y, z, other)
    y_right, y_left, y_far = (y + 1) % 4, (y + 3) % 4, (y + 2) % 4
    z_right, z_left, z_far = (z + 1) % 4, (z + 3) % 4, (z + 2) % 4
    to_y_right, to_y_left = at(y_right, z, core), at(y_left, z, core)
    to_z_right, to_z_left = at(y, z_right, core), at(y, z_left, core)

    me = head * 2 + core

    def peer(step):
        there = (me + step) % PEERS
        return ((y * 4 + z) * 2 + there % 2, there // 2), there // 2, there % 2, there

    def rows(start, size):
        return pl.ds(pl.multiple_of(start, size), size)

    def lanes(index):
        return pl.ds(pl.multiple_of(index * WIDTH, WIDTH), WIDTH)

    own_rows = rows(seq * OWN, OWN)
    own_query = rows(COMP_ROWS + core * OWN, OWN)
    my_slots = rows(core * SLOTS + head * TOKENS, TOKENS)

    local = [
        pltpu.make_async_copy(pqkv.at[1:3, :, lanes(core)], kv.at[:, own_rows, :], local_sem.at[0]),
        pltpu.make_async_copy(pqkv.at[0, :, lanes(core)], x.at[0, own_query, :], local_sem.at[1]),
        pltpu.make_async_copy(pgrad.at[:, lanes(core)], x.at[3, own_query, :], local_sem.at[2]),
        pltpu.make_async_copy(
            cqkv.at[:, 0, :, lanes(me)], x.at[0:3, my_slots, :], local_sem.at[3]
        ),
        pltpu.make_async_copy(cgrad.at[0, :, lanes(me)], x.at[3, my_slots, :], local_sem.at[4]),
    ]
    for copy in local:
        copy.start()

    barrier = pltpu.get_barrier_semaphore()
    for step in range(1, PEERS):
        pl.semaphore_signal(barrier, inc=1, device_id=peer(step)[0], device_id_type=MESH)
    for device in (to_y_right, to_y_left, to_z_right, to_z_left):
        pl.semaphore_signal(barrier, inc=1, device_id=device, device_id_type=MESH)

    position = lax.broadcasted_iota(jnp.int32, (1, SLOTS), 1)
    valid = jnp.where((position < lengths[0]) & (mask[...] == 1), 1.0, 0.0)
    v01[core] = jnp.transpose(jnp.broadcast_to(valid, (HEAD_DIM, SLOTS)))

    pl.semaphore_wait(barrier, PEERS - 1 + 4)

    remote(
        pqkv.at[1:3, :, lanes(other)], kv.at[:, own_rows, :], pair_send.at[0], pair_recv.at[0], partner
    )
    remote(
        pqkv.at[0, :, lanes(other)], x.at[0, own_query, :], pair_send.at[1], pair_recv.at[1], partner
    )
    remote(
        pgrad.at[:, lanes(other)], x.at[3, own_query, :], pair_send.at[2], pair_recv.at[2], partner
    )
    remote(v01.at[core], v01.at[core], pair_send.at[3], pair_recv.at[3], partner)

    def swap(group):
        def body(step, carry):
            device, _, _, there = peer(step)
            if group == 0:
                src, dst = cqkv.at[0, 0, :, lanes(there)], x.at[0, my_slots, :]
            elif group == 1:
                src, dst = cqkv.at[1:3, 0, :, lanes(there)], x.at[1:3, my_slots, :]
            else:
                src, dst = cgrad.at[0, :, lanes(there)], x.at[3, my_slots, :]
            remote(src, dst, swap_send.at[group], swap_recv.at[group], device)
            return carry

        lax.fori_loop(1, PEERS, body, 0)

    def block_at(yy, zz):
        return (yy * 4 + zz) * BLOCK

    def ag(src_start, size, slot, device):
        part = kv.at[:, rows(src_start, size), :]
        remote(part, part, ag_send.at[slot], ag_recv.at[slot], device)

    def ag_wait(start, size, slot):
        await_bytes(kv.at[:, rows(start, size), :], ag_recv.at[slot])

    swap(0)
    local[0].wait()
    await_bytes(kv.at[:, own_rows, :], pair_recv.at[0])
    zs = (z, z_left, z_right, z_far)

    def y_send(j):
        ag(block_at(y, zs[j]), BLOCK, 4 + 4 * j, to_y_right)
        ag(block_at(y, zs[j]), BLOCK, 5 + 4 * j, to_y_left)

    def y_forward(j):
        ag_wait(block_at(y_left, zs[j]), BLOCK, 4 + 4 * j)
        ag(block_at(y_left, zs[j]), OWN, 6 + 4 * j, to_y_right)
        ag_wait(block_at(y_right, zs[j]), BLOCK, 5 + 4 * j)
        ag(block_at(y_right, zs[j]) + OWN, OWN, 7 + 4 * j, to_y_left)

    ag(block_at(y, z), BLOCK, 0, to_z_right)
    ag(block_at(y, z), BLOCK, 1, to_z_left)
    y_send(0)
    swap(2)
    swap(1)
    ag_wait(block_at(y, z_left), BLOCK, 0)
    ag(block_at(y, z_left), OWN, 2, to_z_right)
    ag_wait(block_at(y, z_right), BLOCK, 1)
    ag(block_at(y, z_right) + OWN, OWN, 3, to_z_left)
    y_send(1)
    y_send(2)
    y_forward(0)
    ag_wait(block_at(y, z_far), OWN, 2)
    ag_wait(block_at(y, z_far) + OWN, OWN, 3)
    y_send(3)
    y_forward(1)
    y_forward(2)
    y_forward(3)
    for j in range(4):
        ag_wait(block_at(y_far, zs[j]), OWN, 6 + 4 * j)
        ag_wait(block_at(y_far, zs[j]) + OWN, OWN, 7 + 4 * j)

    for copy in local[1:]:
        copy.wait()
    for slot in (1, 2):
        await_bytes(x.at[0, own_query, :], pair_recv.at[slot])
    await_bytes(v01.at[other], pair_recv.at[3])
    part = (PEERS - 1) * TOKENS
    await_bytes(x.at[0, 0:part, :], swap_recv.at[0])
    await_bytes(x.at[1:3, 0:part, :], swap_recv.at[1])
    await_bytes(x.at[3, 0:part, :], swap_recv.at[2])

    def head_lanes(h):
        return slice(h * HEAD_DIM, (h + 1) * HEAD_DIM)

    def slots_of(comp):
        return slice(comp * SLOTS, (comp + 1) * SLOTS)

    for h in range(2):
        hs = head_lanes(h)
        query = x[0, :, hs]

        def scores(step, top):
            keys = kv[0, rows(step * STEP, STEP), hs]
            score = dot_nt(keys, query)
            e[h, rows(step * STEP, STEP), :] = score
            return jnp.maximum(top, fold_rows(score, jnp.max))

        top = lax.fori_loop(0, PROMPT // STEP, scores, jnp.full((8, ROWS), MASKED, F32))
        near_top = []
        for comp in range(2):
            near = dot_nt(x[1, slots_of(comp), hs], x[0, slots_of(comp), hs])
            okay = v01[comp] > 0.5
            near = jnp.where(jnp.concatenate([okay, okay], axis=1), near, MASKED)
            en[h, slots_of(comp), :] = near
            near_top.append(fold_rows(near, jnp.max))
        near_top.append(jnp.full((8, BLOCK), MASKED, F32))
        top = jnp.maximum(top, jnp.concatenate(near_top, axis=1))
        top = jnp.max(top, axis=0, keepdims=True) * EXP2_FACTOR

        def exps(step, total):
            at_step = rows(step * STEP, STEP)
            grown = jnp.exp2(e[h, at_step, :] * EXP2_FACTOR - top)
            e[h, at_step, :] = grown
            eb[h, at_step, :] = grown.astype(BF16)
            return total + fold_rows(grown, jnp.sum)

        total = lax.fori_loop(0, PROMPT // STEP, exps, jnp.zeros((8, ROWS), F32))
        near_total = []
        for comp in range(2):
            cols = slots_of(comp)
            grown = jnp.exp2(en[h, cols, :] * EXP2_FACTOR - top[:, cols])
            en[h, cols, :] = grown
            enb[h, cols, :] = grown.astype(BF16)
            near_total.append(fold_rows(grown, jnp.sum))
        near_total.append(jnp.zeros((8, BLOCK), F32))
        total = total + jnp.concatenate(near_total, axis=1)
        inverse = 1.0 / jnp.sum(total, axis=0, keepdims=True)

        ot[...] = jnp.zeros_like(ot)

        def outs(step, carry):
            at_step = rows(step * STEP, STEP)
            ot[...] += dot_tn(kv[1, at_step, hs], eb[h, at_step, :])
            return carry

        lax.fori_loop(0, PROMPT // STEP, outs, 0)
        for comp in range(2):
            cols = slots_of(comp)
            ot[:, cols] += dot_tn(x[2, cols, hs], enb[h, cols, :])
        out = (ot[...] * inverse).astype(BF16).astype(F32)
        y_buf[3, :, hs] = jnp.transpose(out).astype(BF16)
        cot = [x[3, slots_of(comp), hs].astype(F32) * v01[comp] for comp in range(2)]
        cot = jnp.concatenate(cot + [x[3, COMP_ROWS:ROWS, hs].astype(F32)], axis=0)
        scaled = (jnp.transpose(cot) * inverse).astype(BF16).astype(F32)
        gp[:, hs] = jnp.transpose(scaled).astype(BF16)
        dl[h] = jnp.broadcast_to(jnp.sum(scaled * out, axis=0, keepdims=True), (8, ROWS))
        dqt[h] = jnp.zeros((HEAD_DIM, ROWS), F32)

    def back(group):
        def body(step, carry):
            device, there_head, there_core, _ = peer(step)
            slots = rows(there_core * SLOTS + there_head * TOKENS, TOKENS)
            if group == 0:
                src, dst = y_buf.at[3, slots, :], cout.at[0, :, lanes(me)]
            elif group == 1:
                src, dst = y_buf.at[1:3, slots, :], cdqkv.at[1:3, 0, :, lanes(me)]
            else:
                src, dst = y_buf.at[0, slots, :], cdqkv.at[0, 0, :, lanes(me)]
            remote(src, dst, back_send.at[group], back_recv.at[group], device)
            return carry

        lax.fori_loop(1, PEERS, body, 0)

    back(0)

    def gradients(yy):
        for h in range(2):
            hs = head_lanes(h)

            def body(step, carry):
                at_step = rows(yy * CHUNK + step * STEP, STEP)
                grad = dot_nt(kv[1, at_step, hs], gp[:, hs])
                ds = (e[h, at_step, :] * (grad - dl[h, 0:1, :])).astype(BF16)
                dp[0, at_step, hs] = dot_nn(ds, x[0, :, hs]).astype(BF16)
                dp[1, at_step, hs] = dot_nn(eb[h, at_step, :], gp[:, hs]).astype(BF16)
                dqt[h] += dot_tn(kv[0, at_step, hs], ds)
                return carry

            lax.fori_loop(0, CHUNK // STEP, body, 0)

    def rs(part, dst, slot, device):
        remote(part, dst, rs_send.at[slot], rs_recv.at[slot], device)

    def add_in(start, size, *arrived):
        width = min(size, 128)

        def body(step, carry):
            at_step = rows(start + step * width, width)
            there = rows(step * width, width)
            total = dp[:, at_step, :].astype(F32)
            for ref in arrived:
                total = total + ref[:, there, :].astype(F32)
            dp[:, at_step, :] = total.astype(BF16)
            return carry

        lax.fori_loop(0, size // width, body, 0)

    def dp_rows(start, size):
        return dp.at[:, rows(start, size), :]

    gradients(y_far)
    rs(dp_rows(y_far * CHUNK, HALF), ra, 0, to_y_right)
    rs(dp_rows(y_far * CHUNK + HALF, HALF), rb, 1, to_y_left)

    for h in range(2):
        hs = head_lanes(h)
        for comp in range(2):
            cols = slots_of(comp)
            grad = dot_nt(x[2, cols, hs], gp[cols, hs])
            ds = (en[h, cols, :] * (grad - dl[h, 0:1, cols])).astype(BF16)
            y_buf[1, cols, hs] = (dot_nn(ds, x[0, cols, hs]) * FACTOR).astype(BF16)
            y_buf[2, cols, hs] = dot_nn(enb[h, cols, :], gp[cols, hs]).astype(BF16)
            dqt[h, :, cols] += dot_tn(x[1, cols, hs], ds)
    back(1)

    gradients(y_right)
    rs(dp_rows(y_right * CHUNK + HALF, HALF), rc.at[:, HALF:CHUNK, :], 3, to_y_right)
    await_bytes(ra, rs_recv.at[0])
    add_in(y_right * CHUNK, HALF, ra)
    rs(dp_rows(y_right * CHUNK, HALF), rc.at[:, 0:HALF, :], 2, to_y_right)
    gradients(y_left)
    rs(dp_rows(y_left * CHUNK, HALF), rd.at[:, 0:HALF, :], 4, to_y_left)
    await_bytes(rb, rs_recv.at[1])
    add_in(y_left * CHUNK + HALF, HALF, rb)
    rs(dp_rows(y_left * CHUNK + HALF, HALF), rd.at[:, HALF:CHUNK, :], 5, to_y_left)
    gradients(y)

    for h in range(2):
        y_buf[0, :, head_lanes(h)] = jnp.transpose(dqt[h] * FACTOR).astype(BF16)
    back(2)

    partner_query = rows(COMP_ROWS + other * OWN, OWN)
    my_half = lanes(core)
    remote(
        y_buf.at[3, partner_query, :], pout.at[:, my_half], last_send.at[0], last_recv.at[0], partner
    )
    remote(
        y_buf.at[0, partner_query, :], pdqkv.at[0, :, my_half], last_send.at[1], last_recv.at[1], partner
    )
    final = [
        pltpu.make_async_copy(y_buf.at[3, own_query, :], pout.at[:, my_half], local_sem.at[0]),
        pltpu.make_async_copy(y_buf.at[0, own_query, :], pdqkv.at[0, :, my_half], local_sem.at[1]),
        pltpu.make_async_copy(
            y_buf.at[0:3, my_slots, :], cdqkv.at[:, 0, :, lanes(me)], local_sem.at[2]
        ),
        pltpu.make_async_copy(y_buf.at[3, my_slots, :], cout.at[0, :, lanes(me)], local_sem.at[3]),
    ]
    for copy in final:
        copy.start()

    await_bytes(rc.at[:, HALF:CHUNK, :], rs_recv.at[3])
    await_bytes(rd.at[:, 0:HALF, :], rs_recv.at[4])
    await_bytes(rc.at[:, 0:HALF, :], rs_recv.at[2])
    await_bytes(rd.at[:, HALF:CHUNK, :], rs_recv.at[5])
    add_in(y * CHUNK, CHUNK, rc, rd)

    rs(dp_rows(block_at(y, z_far), OWN), za, 6, to_z_right)
    rs(dp_rows(block_at(y, z_far) + OWN, OWN), zb, 7, to_z_left)
    await_bytes(za, rs_recv.at[6])
    add_in(block_at(y, z_right), OWN, za)
    rs(dp_rows(block_at(y, z_right), BLOCK), zc, 8, to_z_right)
    await_bytes(zb, rs_recv.at[7])
    add_in(block_at(y, z_left) + OWN, OWN, zb)
    rs(dp_rows(block_at(y, z_left), BLOCK), zd, 9, to_z_left)
    await_bytes(zc, rs_recv.at[8])
    await_bytes(zd, rs_recv.at[9])
    mine = rows(block_at(y, z), BLOCK)
    total = dp[:, mine, :].astype(F32) + zc[...].astype(F32) + zd[...].astype(F32)
    dp[0, mine, :] = (total[0] * FACTOR).astype(BF16)
    dp[1, mine, :] = total[1].astype(BF16)
    partner_rows = rows(block_at(y, z) + other * OWN, OWN)
    remote(
        dp.at[:, partner_rows, :], pdqkv.at[1:3, :, my_half], last_send.at[2], last_recv.at[2], partner
    )
    last = pltpu.make_async_copy(dp.at[:, own_rows, :], pdqkv.at[1:3, :, my_half], local_sem.at[4])
    last.start()

    other_half = lanes(other)
    for slot in range(20):
        size = BLOCK if slot < 2 or (slot >= 4 and slot % 4 < 2) else OWN
        await_bytes(kv.at[:, 0:size, :], ag_send.at[slot])
    for slot, size in enumerate((HALF,) * 6 + (OWN, OWN, BLOCK, BLOCK)):
        await_bytes(dp.at[:, 0:size, :], rs_send.at[slot])
    await_bytes(kv.at[:, own_rows, :], pair_send.at[0])
    for slot in (1, 2):
        await_bytes(x.at[0, own_query, :], pair_send.at[slot])
    await_bytes(v01.at[core], pair_send.at[3])
    for group, ref in enumerate((x.at[0, 0:part, :], x.at[1:3, 0:part, :], x.at[3, 0:part, :])):
        await_bytes(ref, swap_send.at[group])
    for group, ref in enumerate(
        (y_buf.at[3, 0:part, :], y_buf.at[1:3, 0:part, :], y_buf.at[0, 0:part, :])
    ):
        await_bytes(ref, back_send.at[group])
        await_bytes(ref, back_recv.at[group])
    await_bytes(pout.at[:, other_half], last_send.at[0])
    await_bytes(pout.at[:, other_half], last_recv.at[0])
    await_bytes(pdqkv.at[0, :, other_half], last_send.at[1])
    await_bytes(pdqkv.at[0, :, other_half], last_recv.at[1])
    await_bytes(pdqkv.at[1:3, :, other_half], last_send.at[2])
    await_bytes(pdqkv.at[1:3, :, other_half], last_recv.at[2])
    for copy in final:
        copy.wait()
    last.wait()


def local(prompt_qkv, prompt_grad, comp_qkv, comp_grad, lengths, keep_mask):
    hbm = pl.BlockSpec(memory_space=pl.ANY)
    vmem = pltpu.VMEM
    dma = pltpu.SemaphoreType.DMA
    return pl.pallas_call(
        kernel,
        out_shape=(
            jax.ShapeDtypeStruct((OWN, 2 * WIDTH), BF16),
            jax.ShapeDtypeStruct((1, TOKENS, PEERS * WIDTH), BF16),
            jax.ShapeDtypeStruct((3, OWN, 2 * WIDTH), BF16),
            jax.ShapeDtypeStruct((3, 1, TOKENS, PEERS * WIDTH), BF16),
        ),
        in_specs=[
            hbm,
            hbm,
            hbm,
            hbm,
            pl.BlockSpec(memory_space=pltpu.SMEM),
            pl.BlockSpec(memory_space=pltpu.VMEM),
        ],
        out_specs=(hbm, hbm, hbm, hbm),
        scratch_shapes=[
            vmem((2, PROMPT, WIDTH), BF16),
            vmem((4, ROWS, WIDTH), BF16),
            vmem((2, SLOTS, HEAD_DIM), F32),
            vmem((2, PROMPT, ROWS), F32),
            vmem((2, PROMPT, ROWS), BF16),
            vmem((2, COMP_ROWS, SLOTS), F32),
            vmem((2, COMP_ROWS, SLOTS), BF16),
            vmem((HEAD_DIM, ROWS), F32),
            vmem((2, HEAD_DIM, ROWS), F32),
            vmem((ROWS, WIDTH), BF16),
            vmem((2, 8, ROWS), F32),
            vmem((2, PROMPT, WIDTH), BF16),
            vmem((4, ROWS, WIDTH), BF16),
            vmem((2, HALF, WIDTH), BF16),
            vmem((2, HALF, WIDTH), BF16),
            vmem((2, CHUNK, WIDTH), BF16),
            vmem((2, CHUNK, WIDTH), BF16),
            vmem((2, OWN, WIDTH), BF16),
            vmem((2, OWN, WIDTH), BF16),
            vmem((2, BLOCK, WIDTH), BF16),
            vmem((2, BLOCK, WIDTH), BF16),
            dma((5,)),
            dma((4,)),
            dma((4,)),
            dma((3,)),
            dma((3,)),
            dma((20,)),
            dma((20,)),
            dma((10,)),
            dma((10,)),
            dma((3,)),
            dma((3,)),
            dma((3,)),
            dma((3,)),
        ],
        compiler_params=pltpu.CompilerParams(
            collective_id=0, has_side_effects=True, vmem_limit_bytes=56 * 1024 * 1024
        ),
        name="attention",
    )(prompt_qkv, prompt_grad, comp_qkv, comp_grad, lengths, keep_mask)


def solution(mesh):
    in_specs = (
        P(None, "seq", "head"),
        P("seq", "head"),
        P(None, "seq", "head", None),
        P("seq", "head", None),
        P("seq"),
        P("seq", None),
    )
    out_specs = (
        P("seq", "head"),
        P("seq", "head", None),
        P(None, "seq", "head"),
        P(None, "seq", "head", None),
    )
    return jax.shard_map(local, mesh=mesh, in_specs=in_specs, out_specs=out_specs, check_vma=False)
```

time: 277 us -> 97.7 us (0.35); the launches traced: 274 us -> 97.6 us
  Pallas kernels: 0 us -> 90.5 us
  local copies, waits for them, and re-layouts: 94.8 us -> 5.71 us
  waiting for transfers between devices: 66 us -> 0 us
  matrix products: 38.9 us -> 0 us
  other arithmetic: 38.3 us -> 0 us
  starting transfers between devices: 20.6 us -> 0 us
  between operations: 15.1 us -> 1.3 us
    pallas_call x0 -> x1, Pallas kernels: none -> 90.5 us  [local(): pl.pallas_call(kernel, out_shape=(jax.ShapeDtypeStruct((OWN, 2 * WIDTH),...]
    reduce_scatter x1 -> x0, waiting for transfers between devices: 44.4 us -> none  [local(): lax.psum_scatter(jnp.concatenate([dkeys.reshape(count, -1), dvalues.resha...]
    unnamed x42 -> x6, local copies, waits for them, and re-layouts: 49.4 us -> 5.71 us
    dot_general x18 -> x0, matrix products: 38.9 us -> none  [the longest x1 7.81 us: local(): jnp.einsum('chlp,clhe->phe', weight_far, comp_cot, preferred_element_type...]
    unnamed x2 -> x0, other arithmetic: 26.3 us -> none
    all_to_all x4 -> x0, waiting for transfers between devices: 21.6 us -> none  [the longest x1 11.3 us: local(): lax.all_to_all(comp_qkv, 'head', split_axis=3, concat_axis=2, tiled=True)]
    all_to_all x4 -> x0, starting transfers between devices: 20.4 us -> none  [the longest x1 6.2 us: local(): lax.all_to_all(comp_grad[None], 'head', split_axis=3, concat_axis=2, tile...]
    slice x8 -> x0, local copies, waits for them, and re-layouts: 11.2 us -> none  [the longest x1 9.98 us: local(): prompt_keys = gathered[0].reshape(-1, local_heads, HEAD_DIM)]
  transfers between devices with their start and end apart: 6 -> 0, of which waited for: 3 -> 0; matrix products, arithmetic and copies ran while one was open for 34% -> 0% of each run, Pallas kernels for 0% -> 0%
where the time goes in v1:
time: 97.7 us; the launch traced here: 97.6 us
  Pallas kernels  90.5 us (93%)
  local copies, waits for them, and re-layouts  5.71 us (6%)
  between operations  1.3 us (1%)
    pallas_call x1, Pallas kernels, local(): pl.pallas_call(kernel, out_shape=(jax.ShapeDtypeStruct((OWN, 2 * WIDTH),...  90.5 us
    unnamed x6, local copies, waits for them, and re-layouts  5.71 us

profile of v1, /device:TPU:1, one launch (start us, length us, event | category | flops | bytes accessed | tf_op | source)
XLA Modules:
  0.0 97.6 jit_solution(13595925093675072238)
XLA Ops:
  1.3 90.5 %attention.1 = (bf16[64,512]{1,0:T(8,128)(2,1)}, bf16[1,32,4096]{2,1,0:T(8,128)(2,1)}, bf16[3,64,512]{2,1,0:T(8,128)(2,1)}, bf16[3,1,32,4096]{3,2,1,0:T(8,128)(2,1)}) custom-call(bf16[3,64,512]{2,1,0:T(8,128)(2,1)} %pqkv.1, bf16[64,512]{1,0:T(8,128)(2,1)} %pgrad.1, bf16[3,1,32,4096]{3,2,1,0:T(8,128)(2,1)} %cqkv.1, bf16[1,32,4096]{2,1,0:T(8,128)(2,1)} %cgrad.1, ...), custom_call_target="tpu_custom_call" | custom-call | tf_op jit(solution)/shard_map/attention/pallas_call | solution.py:438
  91.8 0.0 copy-start
  91.8 1.5 %copy.15 = bf16[64,512]{1,0:T(8,128)(2,1)} copy(bf16[64,512]{1,0:T(8,128)(2,1)} %get-tuple-element.8) | data formatting | bytes 131072
  93.4 1.7 %copy.16 = bf16[1,32,4096]{2,1,0:T(8,128)(2,1)} copy(bf16[1,32,4096]{2,1,0:T(8,128)(2,1)} %get-tuple-element.9) | data formatting | bytes 524288
  95.1 1.6 %copy.17 = bf16[3,64,512]{2,1,0:T(8,128)(2,1)} copy(bf16[3,64,512]{2,1,0:T(8,128)(2,1)} %get-tuple-element.10) | data formatting | bytes 393216
  96.7 0.0 copy-done
  96.7 0.9 copy.18
Async XLA Ops:
  91.8 4.8 %copy-start = (bf16[3,1,32,4096]{3,2,1,0:T(8,128)(2,1)S(1)}, bf16[3,1,32,4096]{3,2,1,0:T(8,128)(2,1)}, u32[]{:S(2)}) copy-start(bf16[3,1,32,4096]{3,2,1,0:T(8,128)(2,1)} %get-tuple-element.11) | copy-start | bytes 2359300

commit v2 on v1

v2 whole, which is shorter than its diff:
```python
import math

import jax
import jax.numpy as jnp
from jax import lax
from jax.experimental import pallas as pl
from jax.experimental.pallas import tpu as pltpu
from jax.sharding import PartitionSpec as P

MESH = pl.DeviceIdType.MESH
BF16 = jnp.bfloat16
F32 = jnp.float32

HEAD_DIM = 128
FACTOR = 1.0 / math.sqrt(HEAD_DIM)
EXP2_FACTOR = FACTOR * math.log2(math.e)
MASKED = -1e30

SLOTS = 256
COMP_ROWS = 2 * SLOTS
OWN = 64
BLOCK = 2 * OWN
ROWS = COMP_ROWS + BLOCK
WIDTH = 256
PROMPT = 2048
CHUNK = 512
STEP = 256
TOKENS = 32
PEERS = 16


def dot_nt(a, b):
    return lax.dot_general(a, b, (((1,), (1,)), ((), ())), preferred_element_type=F32)


def dot_nn(a, b):
    return lax.dot_general(a, b, (((1,), (0,)), ((), ())), preferred_element_type=F32)


def dot_tn(a, b):
    return lax.dot_general(a, b, (((0,), (0,)), ((), ())), preferred_element_type=F32)


def fold_rows(value, op):
    return op(value.reshape(value.shape[0] // 8, 8, value.shape[1]), axis=0)


def await_bytes(ref, sem):
    pltpu.make_async_copy(ref, ref, sem).wait()


def remote(src, dst, send_sem, recv_sem, device):
    copy = pltpu.make_async_remote_copy(
        src_ref=src,
        dst_ref=dst,
        send_sem=send_sem,
        recv_sem=recv_sem,
        device_id=device,
        device_id_type=MESH,
    )
    copy.start()


def kernel(
    pqkv, pgrad, cqkv, cgrad, lengths, mask,
    pout, cout, pdqkv, cdqkv,
    kv, x, v01, e, eb, en, enb, dsb, tops, ot, gp, dl, dp, y_buf, ra, rb, rc, rd, za, zb, zc, zd,
    local_sem, pair_send, pair_recv, swap_send, swap_recv, ag_send, ag_recv,
    rs_send, rs_recv, back_send, back_recv, last_send, last_recv,
):
    seq = lax.axis_index("seq")
    head = lax.axis_index("head")
    y = seq // 8
    z = (seq // 2) % 4
    core = seq % 2
    other = 1 - core

    def at(yy, zz, cc):
        return ((yy * 4 + zz) * 2 + cc, head)

    partner = at(y, z, other)
    y_right, y_left, y_far = (y + 1) % 4, (y + 3) % 4, (y + 2) % 4
    z_right, z_left, z_far = (z + 1) % 4, (z + 3) % 4, (z + 2) % 4
    to_y_right, to_y_left = at(y_right, z, core), at(y_left, z, core)
    to_z_right, to_z_left = at(y, z_right, core), at(y, z_left, core)

    me = head * 2 + core

    def peer(step):
        there = (me + step) % PEERS
        return ((y * 4 + z) * 2 + there % 2, there // 2), there // 2, there % 2, there

    def rows(start, size):
        return pl.ds(pl.multiple_of(start, size), size)

    def lanes(index):
        return pl.ds(pl.multiple_of(index * WIDTH, WIDTH), WIDTH)

    own_rows = rows(seq * OWN, OWN)
    own_query = rows(COMP_ROWS + core * OWN, OWN)
    my_slots = rows(core * SLOTS + head * TOKENS, TOKENS)

    local = [
        pltpu.make_async_copy(pqkv.at[1:3, :, lanes(core)], kv.at[:, own_rows, :], local_sem.at[0]),
        pltpu.make_async_copy(pqkv.at[0, :, lanes(core)], x.at[0, own_query, :], local_sem.at[1]),
        pltpu.make_async_copy(pgrad.at[:, lanes(core)], x.at[3, own_query, :], local_sem.at[2]),
        pltpu.make_async_copy(
            cqkv.at[:, 0, :, lanes(me)], x.at[0:3, my_slots, :], local_sem.at[3]
        ),
        pltpu.make_async_copy(cgrad.at[0, :, lanes(me)], x.at[3, my_slots, :], local_sem.at[4]),
    ]
    for copy in local:
        copy.start()

    barrier = pltpu.get_barrier_semaphore()
    for device in (to_y_right, to_y_left, to_z_right, to_z_left):
        pl.semaphore_signal(barrier, inc=1, device_id=device, device_id_type=MESH)
    for step in range(1, PEERS):
        pl.semaphore_signal(barrier, inc=1, device_id=peer(step)[0], device_id_type=MESH)

    position = lax.broadcasted_iota(jnp.int32, (1, SLOTS), 1)
    valid = jnp.where((position < lengths[0]) & (mask[...] == 1), 1.0, 0.0)
    v01[core] = jnp.transpose(jnp.broadcast_to(valid, (HEAD_DIM, SLOTS)))

    pl.semaphore_wait(barrier, PEERS - 1 + 4)

    for part in range(2):
        remote(
            pqkv.at[1 + part, :, lanes(other)], kv.at[part, own_rows, :],
            pair_send.at[part], pair_recv.at[part], partner,
        )

    def swap(group):
        def body(step, carry):
            device, _, _, there = peer(step)
            if group < 3:
                src = cqkv.at[group, 0, :, lanes(there)]
            else:
                src = cgrad.at[0, :, lanes(there)]
            remote(src, x.at[group, my_slots, :], swap_send.at[group], swap_recv.at[group], device)
            return carry

        lax.fori_loop(1, PEERS, body, 0)

    others = (PEERS - 1) * TOKENS

    def await_swap(group):
        await_bytes(x.at[group, 0:others, :], swap_recv.at[group])

    def block_at(yy, zz):
        return (yy * 4 + zz) * BLOCK

    def ag(t, start, size, slot, device):
        part = kv.at[t, rows(start, size), :]
        remote(part, part, ag_send.at[t, slot], ag_recv.at[t, slot], device)

    def ag_wait(t, start, size, slot):
        await_bytes(kv.at[t, rows(start, size), :], ag_recv.at[t, slot])

    zs = (z, z_left, z_right, z_far)

    def y_send(t, j):
        ag(t, block_at(y, zs[j]), BLOCK, 4 + 4 * j, to_y_right)
        ag(t, block_at(y, zs[j]), BLOCK, 5 + 4 * j, to_y_left)

    def y_forward(t, j):
        ag_wait(t, block_at(y_left, zs[j]), BLOCK, 4 + 4 * j)
        ag(t, block_at(y_left, zs[j]), OWN, 6 + 4 * j, to_y_right)
        ag_wait(t, block_at(y_right, zs[j]), BLOCK, 5 + 4 * j)
        ag(t, block_at(y_right, zs[j]) + OWN, OWN, 7 + 4 * j, to_y_left)

    def z_forward(t):
        ag_wait(t, block_at(y, z_left), BLOCK, 0)
        ag(t, block_at(y, z_left), OWN, 2, to_z_right)
        ag_wait(t, block_at(y, z_right), BLOCK, 1)
        ag(t, block_at(y, z_right) + OWN, OWN, 3, to_z_left)
        y_send(t, 1)
        y_send(t, 2)

    def z_end(t):
        ag_wait(t, block_at(y, z_far), OWN, 2)
        ag_wait(t, block_at(y, z_far) + OWN, OWN, 3)
        y_send(t, 3)

    def y_end(t):
        for j in range(4):
            ag_wait(t, block_at(y_far, zs[j]), OWN, 6 + 4 * j)
            ag_wait(t, block_at(y_far, zs[j]) + OWN, OWN, 7 + 4 * j)

    def head_lanes(h):
        return slice(h * HEAD_DIM, (h + 1) * HEAD_DIM)

    def slots_of(comp):
        return slice(comp * SLOTS, (comp + 1) * SLOTS)

    def scores(yy):
        def body(step, carry):
            at_step = rows(yy * CHUNK + step * STEP, STEP)
            for h in range(2):
                score = dot_nt(kv[0, at_step, head_lanes(h)], x[0, :, head_lanes(h)])
                e[h, at_step, :] = score
                tops[h] = jnp.maximum(tops[h], fold_rows(score, jnp.max))
            return carry

        lax.fori_loop(0, CHUNK // STEP, body, 0)

    swap(0)
    remote(
        pqkv.at[0, :, lanes(other)], x.at[0, own_query, :], pair_send.at[2], pair_recv.at[2], partner
    )
    remote(
        pgrad.at[:, lanes(other)], x.at[3, own_query, :], pair_send.at[3], pair_recv.at[3], partner
    )
    remote(v01.at[core], v01.at[core], pair_send.at[4], pair_recv.at[4], partner)
    local[0].wait()
    for t in range(2):
        await_bytes(kv.at[t, own_rows, :], pair_recv.at[t])
        ag(t, block_at(y, z), BLOCK, 0, to_z_right)
        ag(t, block_at(y, z), BLOCK, 1, to_z_left)
        y_send(t, 0)
    tops[...] = jnp.full(tops.shape, MASKED, F32)
    z_forward(0)
    y_forward(0, 0)
    z_forward(1)
    swap(1)
    y_forward(1, 0)
    z_end(0)
    y_forward(0, 1)
    y_forward(0, 2)
    z_end(1)
    swap(3)
    swap(2)
    for copy in local[1:]:
        copy.wait()
    for slot in (2, 3):
        await_bytes(x.at[0, own_query, :], pair_recv.at[slot])
    await_bytes(v01.at[other], pair_recv.at[4])
    await_swap(0)
    scores(y)
    y_forward(1, 1)
    y_forward(1, 2)
    y_forward(0, 3)
    scores(y_right)
    y_forward(1, 3)
    scores(y_left)
    y_end(0)
    scores(y_far)

    await_swap(1)
    inverses = []
    for h in range(2):
        hs = head_lanes(h)
        near_top = []
        for comp in range(2):
            near = dot_nt(x[1, slots_of(comp), hs], x[0, slots_of(comp), hs])
            okay = v01[comp] > 0.5
            near = jnp.where(jnp.concatenate([okay, okay], axis=1), near, MASKED)
            en[h, slots_of(comp), :] = near
            near_top.append(fold_rows(near, jnp.max))
        near_top.append(jnp.full((8, BLOCK), MASKED, F32))
        top = jnp.maximum(tops[h], jnp.concatenate(near_top, axis=1))
        top = jnp.max(top, axis=0, keepdims=True) * EXP2_FACTOR

        def exps(step, total):
            at_step = rows(step * STEP, STEP)
            grown = jnp.exp2(e[h, at_step, :] * EXP2_FACTOR - top)
            e[h, at_step, :] = grown
            eb[h, at_step, :] = grown.astype(BF16)
            return total + fold_rows(grown, jnp.sum)

        total = lax.fori_loop(0, PROMPT // STEP, exps, jnp.zeros((8, ROWS), F32))
        near_total = []
        for comp in range(2):
            cols = slots_of(comp)
            grown = jnp.exp2(en[h, cols, :] * EXP2_FACTOR - top[:, cols])
            en[h, cols, :] = grown
            enb[h, cols, :] = grown.astype(BF16)
            near_total.append(fold_rows(grown, jnp.sum))
        near_total.append(jnp.zeros((8, BLOCK), F32))
        total = total + jnp.concatenate(near_total, axis=1)
        inverses.append(1.0 / jnp.sum(total, axis=0, keepdims=True))

    ot[...] = jnp.zeros_like(ot)

    def outs(j, carry):
        yy = (y + j + j // 2 - 2 * (j // 3)) % 4

        @pl.when(j == 3)
        def _():
            y_end(1)

        for h in range(2):
            at_step = rows(yy * CHUNK, CHUNK)
            ot[h] += dot_tn(kv[1, at_step, head_lanes(h)], eb[h, at_step, :])
        return carry

    lax.fori_loop(0, 4, outs, 0)
    await_swap(2)
    await_swap(3)
    for h in range(2):
        hs = head_lanes(h)
        inverse = inverses[h]
        for comp in range(2):
            cols = slots_of(comp)
            ot[h, :, cols] += dot_tn(x[2, cols, hs], enb[h, cols, :])
        out = (ot[h] * inverse).astype(BF16).astype(F32)
        y_buf[3, :, hs] = jnp.transpose(out).astype(BF16)
        cot = [x[3, slots_of(comp), hs].astype(F32) * v01[comp] for comp in range(2)]
        cot = jnp.concatenate(cot + [x[3, COMP_ROWS:ROWS, hs].astype(F32)], axis=0)
        scaled = (jnp.transpose(cot) * inverse).astype(BF16).astype(F32)
        gp[:, hs] = jnp.transpose(scaled).astype(BF16)
        dl[h] = jnp.broadcast_to(jnp.sum(scaled * out, axis=0, keepdims=True), (8, ROWS))

    def back(group):
        def body(step, carry):
            device, there_head, there_core, _ = peer(step)
            slots = rows(there_core * SLOTS + there_head * TOKENS, TOKENS)
            if group == 0:
                src, dst = y_buf.at[3, slots, :], cout.at[0, :, lanes(me)]
            elif group == 1:
                src, dst = y_buf.at[1:3, slots, :], cdqkv.at[1:3, 0, :, lanes(me)]
            else:
                src, dst = y_buf.at[0, slots, :], cdqkv.at[0, 0, :, lanes(me)]
            remote(src, dst, back_send.at[group], back_recv.at[group], device)
            return carry

        lax.fori_loop(1, PEERS, body, 0)

    def ordered(place, j):
        return (place + 10 - j - j // 2 + 2 * (j // 3)) % 4

    def gradients(start):
        at_step = rows(start, BLOCK)
        for h in range(2):
            hs = head_lanes(h)
            grad = dot_nt(kv[1, at_step, hs], gp[:, hs])
            ds = (e[h, at_step, :] * (grad - dl[h, 0:1, :])).astype(BF16)
            dsb[h, at_step, :] = ds
            dp[0, at_step, hs] = dot_nn(ds, x[0, :, hs]).astype(BF16)
            dp[1, at_step, hs] = dot_nn(eb[h, at_step, :], gp[:, hs]).astype(BF16)

    def dp_rows(start, size):
        return dp.at[:, rows(start, size), :]

    def rs(part, dst, slot, device):
        remote(part, dst, rs_send.at[slot], rs_recv.at[slot], device)

    def add_half(start, arrived):
        at_half = rows(start, OWN)
        dp[:, at_half, :] = (dp[:, at_half, :].astype(F32) + arrived.astype(F32)).astype(BF16)

    z_order = (z_far, z_right, z_left, z)

    def y_first(i):
        far = block_at(y_far, z_order[i])
        rs(dp_rows(far, OWN), ra.at[i], 6 * i, to_y_right)
        rs(dp_rows(far + OWN, OWN), rb.at[i], 6 * i + 1, to_y_left)

    def y_second(i):
        right, left = block_at(y_right, z_order[i]), block_at(y_left, z_order[i])
        rs(dp_rows(right + OWN, OWN), rc.at[i, :, OWN:BLOCK, :], 6 * i + 2, to_y_right)
        rs(dp_rows(left, OWN), rd.at[i, :, 0:OWN, :], 6 * i + 3, to_y_left)

    def y_third(i):
        right, left = block_at(y_right, z_order[i]), block_at(y_left, z_order[i])
        await_bytes(ra.at[i], rs_recv.at[6 * i])
        add_half(right, ra[i])
        rs(dp_rows(right, OWN), rc.at[i, :, 0:OWN, :], 6 * i + 4, to_y_right)
        await_bytes(rb.at[i], rs_recv.at[6 * i + 1])
        add_half(left + OWN, rb[i])
        rs(dp_rows(left + OWN, OWN), rd.at[i, :, OWN:BLOCK, :], 6 * i + 5, to_y_left)

    def y_total(i):
        for slot in (2, 4):
            await_bytes(rc.at[i, :, 0:OWN, :], rs_recv.at[6 * i + slot])
        for slot in (3, 5):
            await_bytes(rd.at[i, :, 0:OWN, :], rs_recv.at[6 * i + slot])
        own = dp[:, rows(block_at(y, z_order[i]), BLOCK), :]
        return own.astype(F32) + rc[i].astype(F32) + rd[i].astype(F32)

    def z_first():
        dp[:, rows(block_at(y, z_far), BLOCK), :] = y_total(0).astype(BF16)
        rs(dp_rows(block_at(y, z_far), OWN), za, 24, to_z_right)
        rs(dp_rows(block_at(y, z_far) + OWN, OWN), zb, 25, to_z_left)

    def near_gradients():
        for h in range(2):
            hs = head_lanes(h)
            for comp in range(2):
                cols = slots_of(comp)
                grad = dot_nt(x[2, cols, hs], gp[cols, hs])
                ds = (en[h, cols, :] * (grad - dl[h, 0:1, cols])).astype(BF16)
                y_buf[1, cols, hs] = (dot_nn(ds, x[0, cols, hs]) * FACTOR).astype(BF16)
                y_buf[2, cols, hs] = dot_nn(enb[h, cols, :], gp[cols, hs]).astype(BF16)
                ot[h, :, cols] = dot_tn(x[1, cols, hs], ds)
            ot[h, :, COMP_ROWS:ROWS] = jnp.zeros((HEAD_DIM, BLOCK), F32)
        back(1)

    events = {}
    for i in range(4):
        events.setdefault(4 * i, []).append(lambda i=i: y_first(i))
        events.setdefault(4 * i + 2, []).append(lambda i=i: y_second(i))
        if i < 3:
            events.setdefault(4 * i + 6, []).append(lambda i=i: y_third(i))
    events[0].append(near_gradients)
    events.setdefault(13, []).append(z_first)

    back(0)

    def gradient_step(step, carry):
        gradients(block_at(ordered(y, step % 4), ordered(z, step // 4)))
        for when, todo in sorted(events.items()):

            @pl.when(step == when)
            def _():
                for event in todo:
                    event()

        return carry

    lax.fori_loop(0, 16, gradient_step, 0)
    y_third(3)

    def query_gradients(step, carry):
        at_step = rows(step * CHUNK, CHUNK)
        for h in range(2):
            ot[h] += dot_tn(kv[0, at_step, head_lanes(h)], dsb[h, at_step, :])
        return carry

    lax.fori_loop(0, 4, query_gradients, 0)
    for h in range(2):
        y_buf[0, :, head_lanes(h)] = jnp.transpose(ot[h] * FACTOR).astype(BF16)
    back(2)

    right_block = block_at(y, z_right)
    dp[:, rows(right_block, BLOCK), :] = y_total(1).astype(BF16)
    await_bytes(za, rs_recv.at[24])
    add_half(right_block, za[...])
    rs(dp_rows(right_block, BLOCK), zc, 26, to_z_right)
    left_block = block_at(y, z_left)
    dp[:, rows(left_block, BLOCK), :] = y_total(2).astype(BF16)
    await_bytes(zb, rs_recv.at[25])
    add_half(left_block + OWN, zb[...])
    rs(dp_rows(left_block, BLOCK), zd, 27, to_z_left)

    partner_query = rows(COMP_ROWS + other * OWN, OWN)
    my_half = lanes(core)
    remote(
        y_buf.at[3, partner_query, :], pout.at[:, my_half], last_send.at[0], last_recv.at[0], partner
    )
    remote(
        y_buf.at[0, partner_query, :], pdqkv.at[0, :, my_half], last_send.at[1], last_recv.at[1], partner
    )
    final = [
        pltpu.make_async_copy(y_buf.at[3, own_query, :], pout.at[:, my_half], local_sem.at[0]),
        pltpu.make_async_copy(y_buf.at[0, own_query, :], pdqkv.at[0, :, my_half], local_sem.at[1]),
        pltpu.make_async_copy(
            y_buf.at[0:3, my_slots, :], cdqkv.at[:, 0, :, lanes(me)], local_sem.at[2]
        ),
        pltpu.make_async_copy(y_buf.at[3, my_slots, :], cout.at[0, :, lanes(me)], local_sem.at[3]),
    ]
    for copy in final:
        copy.start()

    total = y_total(3)
    await_bytes(zc, rs_recv.at[26])
    await_bytes(zd, rs_recv.at[27])
    total = total + zc[...].astype(F32) + zd[...].astype(F32)
    mine = rows(block_at(y, z), BLOCK)
    dp[0, mine, :] = (total[0] * FACTOR).astype(BF16)
    dp[1, mine, :] = total[1].astype(BF16)
    partner_rows = rows(block_at(y, z) + other * OWN, OWN)
    remote(
        dp.at[:, partner_rows, :], pdqkv.at[1:3, :, my_half], last_send.at[2], last_recv.at[2], partner
    )
    last = pltpu.make_async_copy(dp.at[:, own_rows, :], pdqkv.at[1:3, :, my_half], local_sem.at[4])
    last.start()

    other_half = lanes(other)
    for t in range(2):
        for slot in range(20):
            size = BLOCK if slot < 2 or (slot >= 4 and slot % 4 < 2) else OWN
            await_bytes(kv.at[t, 0:size, :], ag_send.at[t, slot])
    for slot in range(28):
        await_bytes(dp.at[:, 0 : OWN if slot < 26 else BLOCK, :], rs_send.at[slot])
    for slot in range(4):
        await_bytes(x.at[0, own_query, :], pair_send.at[slot])
    await_bytes(v01.at[core], pair_send.at[4])
    for group in range(4):
        await_bytes(x.at[group, 0:others, :], swap_send.at[group])
    for group, ref in enumerate(
        (y_buf.at[3, 0:others, :], y_buf.at[1:3, 0:others, :], y_buf.at[0, 0:others, :])
    ):
        await_bytes(ref, back_send.at[group])
        await_bytes(ref, back_recv.at[group])
    await_bytes(pout.at[:, other_half], last_send.at[0])
    await_bytes(pout.at[:, other_half], last_recv.at[0])
    await_bytes(pdqkv.at[0, :, other_half], last_send.at[1])
    await_bytes(pdqkv.at[0, :, other_half], last_recv.at[1])
    await_bytes(pdqkv.at[1:3, :, other_half], last_send.at[2])
    await_bytes(pdqkv.at[1:3, :, other_half], last_recv.at[2])
    for copy in final:
        copy.wait()
    last.wait()


def place(*refs):
    sources, targets, held, sem = refs[:4], refs[4:8], refs[8:12], refs[12]
    into = [pltpu.make_async_copy(sources[i], held[i], sem.at[0, i]) for i in range(4)]
    out = [pltpu.make_async_copy(held[i], targets[i], sem.at[1, i]) for i in range(4)]
    for copy in into:
        copy.start()
    for i in range(4):
        into[i].wait()
        out[i].start()
    for copy in out:
        copy.wait()


def local(prompt_qkv, prompt_grad, comp_qkv, comp_grad, lengths, keep_mask):
    hbm = pl.BlockSpec(memory_space=pl.ANY)
    vmem = pltpu.VMEM
    dma = pltpu.SemaphoreType.DMA
    results = pl.pallas_call(
        kernel,
        out_shape=(
            jax.ShapeDtypeStruct((OWN, 2 * WIDTH), BF16),
            jax.ShapeDtypeStruct((1, TOKENS, PEERS * WIDTH), BF16),
            jax.ShapeDtypeStruct((3, OWN, 2 * WIDTH), BF16),
            jax.ShapeDtypeStruct((3, 1, TOKENS, PEERS * WIDTH), BF16),
        ),
        in_specs=[
            hbm,
            hbm,
            hbm,
            hbm,
            pl.BlockSpec(memory_space=pltpu.SMEM),
            pl.BlockSpec(memory_space=pltpu.VMEM),
        ],
        out_specs=(hbm, hbm, hbm, hbm),
        scratch_shapes=[
            vmem((2, PROMPT, WIDTH), BF16),
            vmem((4, ROWS, WIDTH), BF16),
            vmem((2, SLOTS, HEAD_DIM), F32),
            vmem((2, PROMPT, ROWS), F32),
            vmem((2, PROMPT, ROWS), BF16),
            vmem((2, COMP_ROWS, SLOTS), F32),
            vmem((2, COMP_ROWS, SLOTS), BF16),
            vmem((2, PROMPT, ROWS), BF16),
            vmem((2, 8, ROWS), F32),
            vmem((2, HEAD_DIM, ROWS), F32),
            vmem((ROWS, WIDTH), BF16),
            vmem((2, 8, ROWS), F32),
            vmem((2, PROMPT, WIDTH), BF16),
            vmem((4, ROWS, WIDTH), BF16),
            vmem((4, 2, OWN, WIDTH), BF16),
            vmem((4, 2, OWN, WIDTH), BF16),
            vmem((4, 2, BLOCK, WIDTH), BF16),
            vmem((4, 2, BLOCK, WIDTH), BF16),
            vmem((2, OWN, WIDTH), BF16),
            vmem((2, OWN, WIDTH), BF16),
            vmem((2, BLOCK, WIDTH), BF16),
            vmem((2, BLOCK, WIDTH), BF16),
            dma((5,)),
            dma((5,)),
            dma((5,)),
            dma((4,)),
            dma((4,)),
            dma((2, 20)),
            dma((2, 20)),
            dma((28,)),
            dma((28,)),
            dma((3,)),
            dma((3,)),
            dma((3,)),
            dma((3,)),
        ],
        compiler_params=pltpu.CompilerParams(
            collective_id=0, has_side_effects=True, vmem_limit_bytes=56 * 1024 * 1024
        ),
        name="attention",
    )(prompt_qkv, prompt_grad, comp_qkv, comp_grad, lengths, keep_mask)
    return pl.pallas_call(
        place,
        out_shape=tuple(jax.ShapeDtypeStruct(r.shape, r.dtype) for r in results),
        in_specs=[hbm] * 4,
        out_specs=(hbm,) * 4,
        scratch_shapes=[vmem(r.shape, r.dtype) for r in results] + [dma((2, 4))],
        compiler_params=pltpu.CompilerParams(vmem_limit_bytes=56 * 1024 * 1024),
        name="place",
    )(*results)


def solution(mesh):
    in_specs = (
        P(None, "seq", "head"),
        P("seq", "head"),
        P(None, "seq", "head", None),
        P("seq", "head", None),
        P("seq"),
        P("seq", None),
    )
    out_specs = (
        P("seq", "head"),
        P("seq", "head", None),
        P(None, "seq", "head"),
        P(None, "seq", "head", None),
    )
    return jax.shard_map(local, mesh=mesh, in_specs=in_specs, out_specs=out_specs, check_vma=False)
```

time: 97.7 us -> 77.3 us (0.79)
  Pallas kernels: 90.5 us -> 75.9 us
  local copies, waits for them, and re-layouts: 5.71 us -> 0 us
    pallas_call x1, Pallas kernels: 90.5 us -> 73.6 us  [local(): pl.pallas_call(kernel, out_shape=(jax.ShapeDtypeStruct((OWN, 2 * WIDTH),...]
    unnamed x6 -> x0, local copies, waits for them, and re-layouts: 5.71 us -> none
    pallas_call x0 -> x1, Pallas kernels: none -> 2.29 us  [local(): pl.pallas_call(place, out_shape=tuple((jax.ShapeDtypeStruct(r.shape, r.dt...]
where the time goes in v2:
time: 77.3 us; the launch traced here: 77.2 us
  Pallas kernels  75.9 us (98%)
  between operations  1.29 us (2%)
    pallas_call x1, Pallas kernels, local(): pl.pallas_call(kernel, out_shape=(jax.ShapeDtypeStruct((OWN, 2 * WIDTH),...  73.6 us
    pallas_call x1, Pallas kernels, local(): pl.pallas_call(place, out_shape=tuple((jax.ShapeDtypeStruct(r.shape, r.dt...  2.29 us

profile of v2, /device:TPU:1, one launch (start us, length us, event | category | flops | bytes accessed | tf_op | source)
XLA Modules:
  0.0 77.2 jit_solution(591382169449992322)
XLA Ops:
  1.3 73.6 %attention.1 = (bf16[64,512]{1,0:T(8,128)(2,1)}, bf16[1,32,4096]{2,1,0:T(8,128)(2,1)}, bf16[3,64,512]{2,1,0:T(8,128)(2,1)}, bf16[3,1,32,4096]{3,2,1,0:T(8,128)(2,1)}) custom-call(bf16[3,64,512]{2,1,0:T(8,128)(2,1)} %pqkv.1, bf16[64,512]{1,0:T(8,128)(2,1)} %pgrad.1, bf16[3,1,32,4096]{3,2,1,0:T(8,128)(2,1)} %cqkv.1, bf16[1,32,4096]{2,1,0:T(8,128)(2,1)} %cgrad.1, ...), custom_call_target="tpu_custom_call" | custom-call | tf_op jit(solution)/shard_map/attention/pallas_call | solution.py:524
  74.9 2.3 %place.1 = (bf16[64,512]{1,0:T(8,128)(2,1)}, bf16[1,32,4096]{2,1,0:T(8,128)(2,1)}, bf16[3,64,512]{2,1,0:T(8,128)(2,1)}, bf16[3,1,32,4096]{3,2,1,0:T(8,128)(2,1)}) custom-call(bf16[64,512]{1,0:T(8,128)(2,1)} %get-tuple-element.8.refs_0_, bf16[1,32,4096]{2,1,0:T(8,128)(2,1)} %get-tuple-element.9.refs_1_, bf16[3,64,512]{2,1,0:T(8,128)(2,1)} %get-tuple-element.10.refs_2_, ...), custom_call_target="tpu_custom_call" | custom-call | tf_op jit(solution)/shard_map/place/pallas_call | solution.py:583

commit v3 on v2

--- a/solution.py
+++ b/solution.py
@@ -1,3 +1,4 @@
+import functools
 import math
 
 import jax
@@ -27,6 +28,7 @@
 STEP = 256
 TOKENS = 32
 PEERS = 16
+SIDE = PEERS // 2
 
 
 def dot_nt(a, b):
@@ -86,9 +88,12 @@
 
     me = head * 2 + core
 
-    def peer(step):
-        there = (me + step) % PEERS
-        return ((y * 4 + z) * 2 + there % 2, there // 2), there // 2, there % 2, there
+    def peer(step, cross):
+        there = (head // 2 * 2 + core + step) % SIDE
+        there_head = there // 2 * 2 + (head + cross) % 2
+        there_core = there % 2
+        device = ((y * 4 + z) * 2 + there_core, there_head)
+        return device, there_head, there_core, there_head * 2 + there_core
 
     def rows(start, size):
         return pl.ds(pl.multiple_of(start, size), size)
@@ -115,8 +120,10 @@
     barrier = pltpu.get_barrier_semaphore()
     for device in (to_y_right, to_y_left, to_z_right, to_z_left):
         pl.semaphore_signal(barrier, inc=1, device_id=device, device_id_type=MESH)
-    for step in range(1, PEERS):
-        pl.semaphore_signal(barrier, inc=1, device_id=peer(step)[0], device_id_type=MESH)
+    for cross in range(2):
+        for step in range(1 - cross, SIDE):
+            device = peer(step, cross)[0]
+            pl.semaphore_signal(barrier, inc=1, device_id=device, device_id_type=MESH)
 
     position = lax.broadcasted_iota(jnp.int32, (1, SLOTS), 1)
     valid = jnp.where((position < lengths[0]) & (mask[...] == 1), 1.0, 0.0)
@@ -130,22 +137,24 @@
             pair_send.at[part], pair_recv.at[part], partner,
         )
 
-    def swap(group):
+    def swap(group, cross):
         def body(step, carry):
-            device, _, _, there = peer(step)
+            device, _, _, there = peer(step, cross)
             if group < 3:
                 src = cqkv.at[group, 0, :, lanes(there)]
             else:
                 src = cgrad.at[0, :, lanes(there)]
-            remote(src, x.at[group, my_slots, :], swap_send.at[group], swap_recv.at[group], device)
+            dst = x.at[group, my_slots, :]
+            remote(src, dst, swap_send.at[cross, group], swap_recv.at[cross, group], device)
             return carry
 
-        lax.fori_loop(1, PEERS, body, 0)
-
-    others = (PEERS - 1) * TOKENS
+        lax.fori_loop(1 - cross, SIDE, body, 0)
+
+    others = ((SIDE - 1) * TOKENS, SIDE * TOKENS)
 
     def await_swap(group):
-        await_bytes(x.at[group, 0:others, :], swap_recv.at[group])
+        for cross in range(2):
+            await_bytes(x.at[group, 0 : others[cross], :], swap_recv.at[cross, group])
 
     def block_at(yy, zz):
         return (yy * 4 + zz) * BLOCK
@@ -169,11 +178,17 @@
         ag_wait(t, block_at(y_right, zs[j]), BLOCK, 5 + 4 * j)
         ag(t, block_at(y_right, zs[j]) + OWN, OWN, 7 + 4 * j, to_y_left)
 
+    def z_send(t):
+        ag(t, block_at(y, z), BLOCK, 0, to_z_right)
+        ag(t, block_at(y, z), BLOCK, 1, to_z_left)
+
     def z_forward(t):
         ag_wait(t, block_at(y, z_left), BLOCK, 0)
         ag(t, block_at(y, z_left), OWN, 2, to_z_right)
         ag_wait(t, block_at(y, z_right), BLOCK, 1)
         ag(t, block_at(y, z_right) + OWN, OWN, 3, to_z_left)
+        if t == 0:
+            z_send(1)
         y_send(t, 1)
         y_send(t, 2)
 
@@ -194,17 +209,14 @@
         return slice(comp * SLOTS, (comp + 1) * SLOTS)
 
     def scores(yy):
-        def body(step, carry):
-            at_step = rows(yy * CHUNK + step * STEP, STEP)
-            for h in range(2):
-                score = dot_nt(kv[0, at_step, head_lanes(h)], x[0, :, head_lanes(h)])
-                e[h, at_step, :] = score
-                tops[h] = jnp.maximum(tops[h], fold_rows(score, jnp.max))
-            return carry
-
-        lax.fori_loop(0, CHUNK // STEP, body, 0)
-
-    swap(0)
+        at_chunk = rows(yy * CHUNK, CHUNK)
+        for h in range(2):
+            score = dot_nt(kv[0, at_chunk, head_lanes(h)], x[0, :, head_lanes(h)])
+            e[h, at_chunk, :] = score
+            tops[h] = jnp.maximum(tops[h], fold_rows(score, jnp.max))
+
+    swap(0, 0)
+    swap(1, 0)
     remote(
         pqkv.at[0, :, lanes(other)], x.at[0, own_query, :], pair_send.at[2], pair_recv.at[2], partner
     )
@@ -213,23 +225,23 @@
     )
     remote(v01.at[core], v01.at[core], pair_send.at[4], pair_recv.at[4], partner)
     local[0].wait()
-    for t in range(2):
-        await_bytes(kv.at[t, own_rows, :], pair_recv.at[t])
-        ag(t, block_at(y, z), BLOCK, 0, to_z_right)
-        ag(t, block_at(y, z), BLOCK, 1, to_z_left)
-        y_send(t, 0)
     tops[...] = jnp.full(tops.shape, MASKED, F32)
+    await_bytes(kv.at[0, own_rows, :], pair_recv.at[0])
+    z_send(0)
+    y_send(0, 0)
+    await_bytes(kv.at[1, own_rows, :], pair_recv.at[1])
+    y_send(1, 0)
     z_forward(0)
+    swap(0, 1)
     y_forward(0, 0)
-    z_forward(1)
-    swap(1)
     y_forward(1, 0)
     z_end(0)
+    swap(1, 1)
+    z_forward(1)
+    swap(3, 0)
+    swap(2, 0)
     y_forward(0, 1)
     y_forward(0, 2)
-    z_end(1)
-    swap(3)
-    swap(2)
     for copy in local[1:]:
         copy.wait()
     for slot in (2, 3):
@@ -237,9 +249,12 @@
     await_bytes(v01.at[other], pair_recv.at[4])
     await_swap(0)
     scores(y)
+    z_end(1)
+    swap(3, 1)
+    swap(2, 1)
+    y_forward(0, 3)
     y_forward(1, 1)
     y_forward(1, 2)
-    y_forward(0, 3)
     scores(y_right)
     y_forward(1, 3)
     scores(y_left)
@@ -280,21 +295,16 @@
         total = total + jnp.concatenate(near_total, axis=1)
         inverses.append(1.0 / jnp.sum(total, axis=0, keepdims=True))
 
-    ot[...] = jnp.zeros_like(ot)
-
-    def outs(j, carry):
-        yy = (y + j + j // 2 - 2 * (j // 3)) % 4
-
-        @pl.when(j == 3)
-        def _():
-            y_end(1)
-
-        for h in range(2):
-            at_step = rows(yy * CHUNK, CHUNK)
-            ot[h] += dot_tn(kv[1, at_step, head_lanes(h)], eb[h, at_step, :])
-        return carry
-
-    lax.fori_loop(0, 4, outs, 0)
+    def outs(first, second, h):
+        values = [kv[1, rows(yy * CHUNK, CHUNK), head_lanes(h)] for yy in (first, second)]
+        weights = [eb[h, rows(yy * CHUNK, CHUNK), :] for yy in (first, second)]
+        return dot_tn(jnp.concatenate(values, axis=0), jnp.concatenate(weights, axis=0))
+
+    for h in range(2):
+        ot[h] = outs(y, y_right, h)
+    y_end(1)
+    for h in range(2):
+        ot[h] += outs(y_left, y_far, h)
     await_swap(2)
     await_swap(3)
     for h in range(2):
@@ -312,8 +322,8 @@
         dl[h] = jnp.broadcast_to(jnp.sum(scaled * out, axis=0, keepdims=True), (8, ROWS))
 
     def back(group):
-        def body(step, carry):
-            device, there_head, there_core, _ = peer(step)
+        def body(cross, step, carry):
+            device, there_head, there_core, _ = peer(step, cross)
             slots = rows(there_core * SLOTS + there_head * TOKENS, TOKENS)
             if group == 0:
                 src, dst = y_buf.at[3, slots, :], cout.at[0, :, lanes(me)]
@@ -324,20 +334,24 @@
             remote(src, dst, back_send.at[group], back_recv.at[group], device)
             return carry
 
-        lax.fori_loop(1, PEERS, body, 0)
-
-    def ordered(place, j):
-        return (place + 10 - j - j // 2 + 2 * (j // 3)) % 4
-
-    def gradients(start):
-        at_step = rows(start, BLOCK)
+        lax.fori_loop(0, SIDE, functools.partial(body, 1), 0)
+        lax.fori_loop(1, SIDE, functools.partial(body, 0), 0)
+
+    def gradients(zz):
+        places = [rows(block_at(yy, zz), BLOCK) for yy in (y_far, y_right, y_left, y)]
         for h in range(2):
             hs = head_lanes(h)
-            grad = dot_nt(kv[1, at_step, hs], gp[:, hs])
-            ds = (e[h, at_step, :] * (grad - dl[h, 0:1, :])).astype(BF16)
-            dsb[h, at_step, :] = ds
-            dp[0, at_step, hs] = dot_nn(ds, x[0, :, hs]).astype(BF16)
-            dp[1, at_step, hs] = dot_nn(eb[h, at_step, :], gp[:, hs]).astype(BF16)
+            values = jnp.concatenate([kv[1, where, hs] for where in places], axis=0)
+            weights = jnp.concatenate([e[h, where, :] for where in places], axis=0)
+            rounded = jnp.concatenate([eb[h, where, :] for where in places], axis=0)
+            ds = (weights * (dot_nt(values, gp[:, hs]) - dl[h, 0:1, :])).astype(BF16)
+            dk = dot_nn(ds, x[0, :, hs]).astype(BF16)
+            dv = dot_nn(rounded, gp[:, hs]).astype(BF16)
+            for i, where in enumerate(places):
+                part = slice(i * BLOCK, (i + 1) * BLOCK)
+                dsb[h, where, :] = ds[part]
+                dp[0, where, hs] = dk[part]
+                dp[1, where, hs] = dv[part]
 
     def dp_rows(start, size):
         return dp.at[:, rows(start, size), :]
@@ -396,41 +410,31 @@
             ot[h, :, COMP_ROWS:ROWS] = jnp.zeros((HEAD_DIM, BLOCK), F32)
         back(1)
 
-    events = {}
-    for i in range(4):
-        events.setdefault(4 * i, []).append(lambda i=i: y_first(i))
-        events.setdefault(4 * i + 2, []).append(lambda i=i: y_second(i))
-        if i < 3:
-            events.setdefault(4 * i + 6, []).append(lambda i=i: y_third(i))
-    events[0].append(near_gradients)
-    events.setdefault(13, []).append(z_first)
-
     back(0)
 
+    def after(step):
+        y_first(step)
+        y_second(step)
+        if step == 0:
+            near_gradients()
+        else:
+            y_third(step - 1)
+        if step == 3:
+            z_first()
+
     def gradient_step(step, carry):
-        gradients(block_at(ordered(y, step % 4), ordered(z, step // 4)))
-        for when, todo in sorted(events.items()):
-
-            @pl.when(step == when)
-            def _():
-                for event in todo:
-                    event()
-
+        gradients((z + 10 - step - step // 2 + 2 * (step // 3)) % 4)
+        for when in range(4):
+            pl.when(step == when)(functools.partial(after, when))
         return carry
 
-    lax.fori_loop(0, 16, gradient_step, 0)
-    y_third(3)
-
-    def query_gradients(step, carry):
-        at_step = rows(step * CHUNK, CHUNK)
-        for h in range(2):
-            ot[h] += dot_tn(kv[0, at_step, head_lanes(h)], dsb[h, at_step, :])
-        return carry
-
-    lax.fori_loop(0, 4, query_gradients, 0)
+    lax.fori_loop(0, 4, gradient_step, 0)
+    for h in range(2):
+        ot[h] += dot_tn(kv[0, :, head_lanes(h)], dsb[h])
     for h in range(2):
         y_buf[0, :, head_lanes(h)] = jnp.transpose(ot[h] * FACTOR).astype(BF16)
     back(2)
+    y_third(3)
 
     right_block = block_at(y, z_right)
     dp[:, rows(right_block, BLOCK), :] = y_total(1).astype(BF16)
@@ -487,9 +491,11 @@
         await_bytes(x.at[0, own_query, :], pair_send.at[slot])
     await_bytes(v01.at[core], pair_send.at[4])
     for group in range(4):
-        await_bytes(x.at[group, 0:others, :], swap_send.at[group])
+        for cross in range(2):
+            await_bytes(x.at[group, 0 : others[cross], :], swap_send.at[cross, group])
+    sent = (PEERS - 1) * TOKENS
     for group, ref in enumerate(
-        (y_buf.at[3, 0:others, :], y_buf.at[1:3, 0:others, :], y_buf.at[0, 0:others, :])
+        (y_buf.at[3, 0:sent, :], y_buf.at[1:3, 0:sent, :], y_buf.at[0, 0:sent, :])
     ):
         await_bytes(ref, back_send.at[group])
         await_bytes(ref, back_recv.at[group])
@@ -564,8 +570,8 @@
             dma((5,)),
             dma((5,)),
             dma((5,)),
-            dma((4,)),
-            dma((4,)),
+            dma((2, 4)),
+            dma((2, 4)),
             dma((2, 20)),
             dma((2, 20)),
             dma((28,)),

time: 77.3 us -> 73 us (0.944)
  Pallas kernels: 75.9 us -> 71.6 us
    pallas_call x1, Pallas kernels: 73.6 us -> 69.3 us  [local(): pl.pallas_call(kernel, out_shape=(jax.ShapeDtypeStruct((OWN, 2 * WIDTH),...]
where the time goes in v3:
time: 73 us; the launch traced here: 72.9 us
  Pallas kernels  71.6 us (98%)
  between operations  1.29 us (2%)
    pallas_call x1, Pallas kernels, local(): pl.pallas_call(kernel, out_shape=(jax.ShapeDtypeStruct((OWN, 2 * WIDTH),...  69.3 us
    pallas_call x1, Pallas kernels, local(): pl.pallas_call(place, out_shape=tuple((jax.ShapeDtypeStruct(r.shape, r.dt...  2.29 us

profile of v3, /device:TPU:1, one launch (start us, length us, event | category | flops | bytes accessed | tf_op | source)
XLA Modules:
  0.0 72.9 jit_solution(13329391812607945852)
XLA Ops:
  1.3 69.3 %attention.1 = (bf16[64,512]{1,0:T(8,128)(2,1)}, bf16[1,32,4096]{2,1,0:T(8,128)(2,1)}, bf16[3,64,512]{2,1,0:T(8,128)(2,1)}, bf16[3,1,32,4096]{3,2,1,0:T(8,128)(2,1)}) custom-call(bf16[3,64,512]{2,1,0:T(8,128)(2,1)} %pqkv.1, bf16[64,512]{1,0:T(8,128)(2,1)} %pgrad.1, bf16[3,1,32,4096]{3,2,1,0:T(8,128)(2,1)} %cqkv.1, bf16[1,32,4096]{2,1,0:T(8,128)(2,1)} %cgrad.1, ...), custom_call_target="tpu_custom_call" | custom-call | tf_op jit(solution)/shard_map/attention/pallas_call | solution.py:530
  70.6 2.3 %place.1 = (bf16[64,512]{1,0:T(8,128)(2,1)}, bf16[1,32,4096]{2,1,0:T(8,128)(2,1)}, bf16[3,64,512]{2,1,0:T(8,128)(2,1)}, bf16[3,1,32,4096]{3,2,1,0:T(8,128)(2,1)}) custom-call(bf16[64,512]{1,0:T(8,128)(2,1)} %get-tuple-element.8.refs_0_, bf16[1,32,4096]{2,1,0:T(8,128)(2,1)} %get-tuple-element.9.refs_1_, bf16[3,64,512]{2,1,0:T(8,128)(2,1)} %get-tuple-element.10.refs_2_, ...), custom_call_target="tpu_custom_call" | custom-call | tf_op jit(solution)/shard_map/place/pallas_call | solution.py:589

commit v4 on v0

v4 whole, which is shorter than its diff:
```python
import functools
import math

import jax
import jax.numpy as jnp
from jax import lax
from jax.experimental import pallas as pl
from jax.experimental.pallas import tpu as pltpu
from jax.sharding import PartitionSpec as P

MESH = pl.DeviceIdType.MESH
BF16 = jnp.bfloat16
F32 = jnp.float32

HEAD_DIM = 128
FACTOR = 1.0 / math.sqrt(HEAD_DIM)
EXP2_FACTOR = FACTOR * math.log2(math.e)
MASKED = -1e30

SLOTS = 256
COMP_ROWS = 2 * SLOTS
OWN = 64
BLOCK = 2 * OWN
ROWS = COMP_ROWS + BLOCK
PROMPT = 2048
CHUNK = 512
STEP = 512
TOKENS = 32
PEERS = 16
SIDE = PEERS // 2


def dot_nt(a, b):
    return lax.dot_general(a, b, (((1,), (1,)), ((), ())), preferred_element_type=F32)


def dot_nn(a, b):
    return lax.dot_general(a, b, (((1,), (0,)), ((), ())), preferred_element_type=F32)


def dot_tn(a, b):
    return lax.dot_general(a, b, (((0,), (0,)), ((), ())), preferred_element_type=F32)


def fold_rows(value, op):
    return op(value.reshape(value.shape[0] // 8, 8, value.shape[1]), axis=0)


def await_bytes(ref, sem):
    pltpu.make_async_copy(ref, ref, sem).wait()


def remote(src, dst, send_sem, recv_sem, device):
    copy = pltpu.make_async_remote_copy(
        src_ref=src,
        dst_ref=dst,
        send_sem=send_sem,
        recv_sem=recv_sem,
        device_id=device,
        device_id_type=MESH,
    )
    copy.start()


def kernel(
    pqkv, pgrad, cqkv, cgrad, lengths, mask,
    pout, cout, pdqkv, cdqkv,
    kv, x, v01, e, eb, en, enb, dsb, tops, ot, inv, gp, dl, dp, y_buf, ra, rb, rc, rd, za, zb, zc, zd,
    local_sem, final_sem, pair_send, pair_recv, swap_send, swap_recv, ag_send, ag_recv,
    rs_send, rs_recv, back_send, back_recv, last_send, last_recv,
):
    seq = lax.axis_index("seq")
    head = lax.axis_index("head")
    y = seq // 8
    z = (seq // 2) % 4
    core = seq % 2
    other = 1 - core

    def at(yy, zz, cc):
        return ((yy * 4 + zz) * 2 + cc, head)

    partner = at(y, z, other)
    y_right, y_left, y_far = (y + 1) % 4, (y + 3) % 4, (y + 2) % 4
    z_right, z_left, z_far = (z + 1) % 4, (z + 3) % 4, (z + 2) % 4
    to_y_right, to_y_left = at(y_right, z, core), at(y_left, z, core)
    to_z_right, to_z_left = at(y, z_right, core), at(y, z_left, core)

    me = head * 2 + core

    def peer(step, cross):
        there = (head // 2 * 2 + core + step) % SIDE
        there_head = there // 2 * 2 + (head + cross) % 2
        there_core = there % 2
        device = ((y * 4 + z) * 2 + there_core, there_head)
        return device, there_head, there_core, there_head * 2 + there_core

    def rows(start, size):
        return pl.ds(pl.multiple_of(start, size), size)

    def lanes(index, h):
        return pl.ds(pl.multiple_of((2 * index + h) * HEAD_DIM, HEAD_DIM), HEAD_DIM)

    own_rows = rows(seq * OWN, OWN)
    own_query = rows(COMP_ROWS + core * OWN, OWN)
    my_slots = rows(core * SLOTS + head * TOKENS, TOKENS)

    local = []
    for h in range(2):
        mine = (
            (pqkv.at[1:3, :, lanes(core, h)], kv.at[h, :, own_rows, :]),
            (pqkv.at[0, :, lanes(core, h)], x.at[h, 0, own_query, :]),
            (pgrad.at[:, lanes(core, h)], x.at[h, 3, own_query, :]),
            (cqkv.at[:, 0, :, lanes(me, h)], x.at[h, 0:3, my_slots, :]),
            (cgrad.at[0, :, lanes(me, h)], x.at[h, 3, my_slots, :]),
        )
        for i, (src, dst) in enumerate(mine):
            local.append(pltpu.make_async_copy(src, dst, local_sem.at[h, i]))
    for copy in local:
        copy.start()

    barrier = pltpu.get_barrier_semaphore()
    around = ((y_right, z), (y_left, z), (y, z_right), (y, z_left))
    for yy, zz in around:
        for cc in range(2):
            pl.semaphore_signal(barrier, inc=1, device_id=at(yy, zz, cc), device_id_type=MESH)
    for cross in range(2):
        for step in range(1 - cross, SIDE):
            device = peer(step, cross)[0]
            pl.semaphore_signal(barrier, inc=1, device_id=device, device_id_type=MESH)

    position = lax.broadcasted_iota(jnp.int32, (1, SLOTS), 1)
    valid = jnp.where((position < lengths[0]) & (mask[...] == 1), 1.0, 0.0)
    v01[core] = jnp.transpose(jnp.broadcast_to(valid, (HEAD_DIM, SLOTS)))

    pl.semaphore_wait(barrier, PEERS - 1 + 8)

    def swap(h, group, cross):
        def body(step, carry):
            device, _, _, there = peer(step, cross)
            if group == 0:
                src, dst = cqkv.at[0:2, 0, :, lanes(there, h)], x.at[h, 0:2, my_slots, :]
            elif group == 1:
                src, dst = cqkv.at[2, 0, :, lanes(there, h)], x.at[h, 2, my_slots, :]
            else:
                src, dst = cgrad.at[0, :, lanes(there, h)], x.at[h, 3, my_slots, :]
            sems = swap_send.at[h, cross, group], swap_recv.at[h, cross, group]
            remote(src, dst, *sems, device)
            return carry

        lax.fori_loop(1 - cross, SIDE, body, 0)

    others = ((SIDE - 1) * TOKENS, SIDE * TOKENS)

    def swapped(h, group, cross):
        arrays = (slice(0, 2), 2, 3)[group]
        return x.at[h, arrays, 0 : others[cross], :]

    def await_swap(h, group):
        for cross in range(2):
            await_bytes(swapped(h, group, cross), swap_recv.at[h, cross, group])

    def block_at(yy, zz):
        return (yy * 4 + zz) * BLOCK

    def held(s, start, size):
        return kv.at[s // 2, s % 2, rows(start, size), :]

    def ag(s, start, size, slot, device):
        part = held(s, start, size)
        remote(part, part, ag_send.at[s, slot], ag_recv.at[s, slot], device)

    def ag_wait(s, start, size, slot):
        await_bytes(held(s, start, size), ag_recv.at[s, slot])

    def own_part(s, device_core, send_slot, recv_sem, device):
        src = pqkv.at[1 + s % 2, :, lanes(device_core, s // 2)]
        remote(src, held(s, seq * OWN, OWN), ag_send.at[s, send_slot], recv_sem, device)

    def own_pair(s):
        remote(
            pqkv.at[1 + s % 2, :, lanes(other, s // 2)], held(s, seq * OWN, OWN),
            pair_send.at[s], pair_recv.at[s], partner,
        )

    def own_z(s):
        for cc in range(2):
            own_part(s, cc, cc, ag_recv.at[s, core], at(y, z_right, cc))
            own_part(s, cc, 2 + cc, ag_recv.at[s, 2 + core], at(y, z_left, cc))

    def own_y(s):
        for cc in range(2):
            own_part(s, cc, 6 + cc, ag_recv.at[s, 6 + core], at(y_right, z, cc))
            own_part(s, cc, 8 + cc, ag_recv.at[s, 8 + core], at(y_left, z, cc))

    zs = (z, z_left, z_right, z_far)

    def y_send(s, j):
        ag(s, block_at(y, zs[j]), BLOCK, 8 + 4 * j, to_y_right)
        ag(s, block_at(y, zs[j]), BLOCK, 9 + 4 * j, to_y_left)

    def z_forward(s):
        left, right = block_at(y, z_left), block_at(y, z_right)
        ag_wait(s, left, OWN, 0)
        ag(s, left, OWN, 4, to_z_right)
        ag_wait(s, right + OWN, OWN, 3)
        ag(s, right + OWN, OWN, 5, to_z_left)
        ag_wait(s, left + OWN, OWN, 1)
        y_send(s, 1)
        ag_wait(s, right, OWN, 2)
        y_send(s, 2)

    def z_end(s):
        ag_wait(s, block_at(y, z_far), OWN, 4)
        ag_wait(s, block_at(y, z_far) + OWN, OWN, 5)
        y_send(s, 3)

    def y_forward(s, j):
        left, right = block_at(y_left, zs[j]), block_at(y_right, zs[j])
        if j == 0:
            ag_wait(s, left, OWN, 6)
            ag(s, left, OWN, 10, to_y_right)
            ag_wait(s, right + OWN, OWN, 9)
            ag(s, right + OWN, OWN, 11, to_y_left)
            ag_wait(s, left + OWN, OWN, 7)
            ag_wait(s, right, OWN, 8)
        else:
            ag_wait(s, left, BLOCK, 8 + 4 * j)
            ag(s, left, OWN, 10 + 4 * j, to_y_right)
            ag_wait(s, right, BLOCK, 9 + 4 * j)
            ag(s, right + OWN, OWN, 11 + 4 * j, to_y_left)

    def y_end(s):
        for j in range(4):
            ag_wait(s, block_at(y_far, zs[j]), OWN, 10 + 4 * j)
            ag_wait(s, block_at(y_far, zs[j]) + OWN, OWN, 11 + 4 * j)

    def slots_of(comp):
        return slice(comp * SLOTS, (comp + 1) * SLOTS)

    def scores(h, yy):
        at_chunk = rows(yy * CHUNK, CHUNK)
        score = dot_nt(kv[h, 0, at_chunk, :], x[h, 0])
        e[h, at_chunk, :] = score
        tops[h] = jnp.maximum(tops[h], fold_rows(score, jnp.max))

    def exponentials(h):
        near_top = []
        for comp in range(2):
            near = dot_nt(x[h, 1, slots_of(comp), :], x[h, 0, slots_of(comp), :])
            okay = v01[comp] > 0.5
            near = jnp.where(jnp.concatenate([okay, okay], axis=1), near, MASKED)
            en[h, slots_of(comp), :] = near
            near_top.append(fold_rows(near, jnp.max))
        near_top.append(jnp.full((8, BLOCK), MASKED, F32))
        top = jnp.maximum(tops[h], jnp.concatenate(near_top, axis=1))
        top = jnp.max(top, axis=0, keepdims=True) * EXP2_FACTOR

        def exps(step, total):
            at_step = rows(step * STEP, STEP)
            grown = jnp.exp2(e[h, at_step, :] * EXP2_FACTOR - top)
            e[h, at_step, :] = grown
            eb[h, at_step, :] = grown.astype(BF16)
            return total + fold_rows(grown, jnp.sum)

        total = lax.fori_loop(0, PROMPT // STEP, exps, jnp.zeros((8, ROWS), F32))
        near_total = []
        for comp in range(2):
            cols = slots_of(comp)
            grown = jnp.exp2(en[h, cols, :] * EXP2_FACTOR - top[:, cols])
            en[h, cols, :] = grown
            enb[h, cols, :] = grown.astype(BF16)
            near_total.append(fold_rows(grown, jnp.sum))
        near_total.append(jnp.zeros((8, BLOCK), F32))
        total = total + jnp.concatenate(near_total, axis=1)
        inverse = 1.0 / jnp.sum(total, axis=0, keepdims=True)
        inv[h] = jnp.broadcast_to(inverse, (8, ROWS))

    def outputs(h):
        inverse = inv[h, 0:1, :]
        ot[h] = dot_tn(kv[h, 1], eb[h])
        await_swap(h, 1)
        await_swap(h, 2)
        for comp in range(2):
            cols = slots_of(comp)
            ot[h, :, cols] += dot_tn(x[h, 2, cols, :], enb[h, cols, :])
        out = (ot[h] * inverse).astype(BF16).astype(F32)
        y_buf[h, 3] = jnp.transpose(out).astype(BF16)
        cot = [x[h, 3, slots_of(comp), :].astype(F32) * v01[comp] for comp in range(2)]
        cot = jnp.concatenate(cot + [x[h, 3, COMP_ROWS:ROWS, :].astype(F32)], axis=0)
        scaled = (jnp.transpose(cot) * inverse).astype(BF16).astype(F32)
        gp[h] = jnp.transpose(scaled).astype(BF16)
        dl[h] = jnp.broadcast_to(jnp.sum(scaled * out, axis=0, keepdims=True), (8, ROWS))
        back(h, 0)

    def back(h, group):
        def body(cross, step, carry):
            device, there_head, there_core, _ = peer(step, cross)
            slots = rows(there_core * SLOTS + there_head * TOKENS, TOKENS)
            if group == 0:
                src, dst = y_buf.at[h, 3, slots, :], cout.at[0, :, lanes(me, h)]
            else:
                src, dst = y_buf.at[h, 0:3, slots, :], cdqkv.at[:, 0, :, lanes(me, h)]
            remote(src, dst, back_send.at[h, group], back_recv.at[h, group], device)
            return carry

        lax.fori_loop(0, SIDE, functools.partial(body, 1), 0)
        lax.fori_loop(1, SIDE, functools.partial(body, 0), 0)

    def gradients(h, zz):
        places = [rows(block_at(yy, zz), BLOCK) for yy in (y_far, y_right, y_left, y)]
        values = jnp.concatenate([kv[h, 1, where, :] for where in places], axis=0)
        weights = jnp.concatenate([e[h, where, :] for where in places], axis=0)
        rounded = jnp.concatenate([eb[h, where, :] for where in places], axis=0)
        ds = (weights * (dot_nt(values, gp[h]) - dl[h, 0:1, :])).astype(BF16)
        dk = dot_nn(ds, x[h, 0]).astype(BF16)
        dv = dot_nn(rounded, gp[h]).astype(BF16)
        for i, where in enumerate(places):
            part = slice(i * BLOCK, (i + 1) * BLOCK)
            dsb[h, where, :] = ds[part]
            dp[h, 0, where, :] = dk[part]
            dp[h, 1, where, :] = dv[part]

    def rest(h):
        for comp in range(2):
            cols = slots_of(comp)
            grad = dot_nt(x[h, 2, cols, :], gp[h, cols, :])
            ds = (en[h, cols, :] * (grad - dl[h, 0:1, cols])).astype(BF16)
            y_buf[h, 1, cols, :] = (dot_nn(ds, x[h, 0, cols, :]) * FACTOR).astype(BF16)
            y_buf[h, 2, cols, :] = dot_nn(enb[h, cols, :], gp[h, cols, :]).astype(BF16)
            ot[h, :, cols] = dot_tn(x[h, 1, cols, :], ds)
        ot[h, :, COMP_ROWS:ROWS] = jnp.zeros((HEAD_DIM, BLOCK), F32)
        total = ot[h] + dot_tn(kv[h, 0], dsb[h])
        y_buf[h, 0] = jnp.transpose(total * FACTOR).astype(BF16)
        back(h, 1)

    def dp_rows(h, start, size):
        return dp.at[h, :, rows(start, size), :]

    def rs(h, part, dst, slot, device):
        remote(part, dst, rs_send.at[h, slot], rs_recv.at[h, slot], device)

    def add_half(h, start, arrived):
        at_half = rows(start, OWN)
        dp[h, :, at_half, :] = (dp[h, :, at_half, :].astype(F32) + arrived.astype(F32)).astype(BF16)

    z_order = (z_far, z_right, z_left, z)

    def y_first(h, i):
        far = block_at(y_far, z_order[i])
        rs(h, dp_rows(h, far, OWN), ra.at[h, i], 6 * i, to_y_right)
        rs(h, dp_rows(h, far + OWN, OWN), rb.at[h, i], 6 * i + 1, to_y_left)

    def y_second(h, i):
        right, left = block_at(y_right, z_order[i]), block_at(y_left, z_order[i])
        rs(h, dp_rows(h, right + OWN, OWN), rc.at[h, i, :, OWN:BLOCK, :], 6 * i + 2, to_y_right)
        rs(h, dp_rows(h, left, OWN), rd.at[h, i, :, 0:OWN, :], 6 * i + 3, to_y_left)

    def y_third(h, i):
        right, left = block_at(y_right, z_order[i]), block_at(y_left, z_order[i])
        await_bytes(ra.at[h, i], rs_recv.at[h, 6 * i])
        add_half(h, right, ra[h, i])
        rs(h, dp_rows(h, right, OWN), rc.at[h, i, :, 0:OWN, :], 6 * i + 4, to_y_right)
        await_bytes(rb.at[h, i], rs_recv.at[h, 6 * i + 1])
        add_half(h, left + OWN, rb[h, i])
        rs(h, dp_rows(h, left + OWN, OWN), rd.at[h, i, :, OWN:BLOCK, :], 6 * i + 5, to_y_left)

    def y_total(h, i):
        for slot in (2, 4):
            await_bytes(rc.at[h, i, :, 0:OWN, :], rs_recv.at[h, 6 * i + slot])
        for slot in (3, 5):
            await_bytes(rd.at[h, i, :, 0:OWN, :], rs_recv.at[h, 6 * i + slot])
        own = dp[h, :, rows(block_at(y, z_order[i]), BLOCK), :]
        return own.astype(F32) + rc[h, i].astype(F32) + rd[h, i].astype(F32)

    def z_first(h):
        far = block_at(y, z_far)
        dp[h, :, rows(far, BLOCK), :] = y_total(h, 0).astype(BF16)
        rs(h, dp_rows(h, far, OWN), za.at[h], 24, to_z_right)
        rs(h, dp_rows(h, far + OWN, OWN), zb.at[h], 25, to_z_left)

    def z_second(h, i):
        block = block_at(y, z_order[i])
        dp[h, :, rows(block, BLOCK), :] = y_total(h, i).astype(BF16)
        if i == 1:
            await_bytes(za.at[h], rs_recv.at[h, 24])
            add_half(h, block, za[h])
            rs(h, dp_rows(h, block, BLOCK), zc.at[h], 26, to_z_right)
        else:
            await_bytes(zb.at[h], rs_recv.at[h, 25])
            add_half(h, block + OWN, zb[h])
            rs(h, dp_rows(h, block, BLOCK), zd.at[h], 27, to_z_left)

    partner_query = rows(COMP_ROWS + other * OWN, OWN)
    partner_rows = rows(block_at(y, z) + other * OWN, OWN)
    final = []

    def keep(h, slot, src, dst):
        final.append(pltpu.make_async_copy(src, dst, final_sem.at[h, slot]))
        final[-1].start()

    def give(h, slot, src, dst):
        remote(src, dst, last_send.at[h, slot], last_recv.at[h, slot], partner)

    def finish_queries(h):
        mine = lanes(core, h)
        give(h, 0, y_buf.at[h, 3, partner_query, :], pout.at[:, mine])
        give(h, 1, y_buf.at[h, 0, partner_query, :], pdqkv.at[0, :, mine])
        keep(h, 0, y_buf.at[h, 3, own_query, :], pout.at[:, mine])
        keep(h, 1, y_buf.at[h, 0, own_query, :], pdqkv.at[0, :, mine])
        keep(h, 2, y_buf.at[h, 0:3, my_slots, :], cdqkv.at[:, 0, :, lanes(me, h)])
        keep(h, 3, y_buf.at[h, 3, my_slots, :], cout.at[0, :, lanes(me, h)])

    def finish_keys(h):
        total = y_total(h, 3)
        await_bytes(zc.at[h], rs_recv.at[h, 26])
        await_bytes(zd.at[h], rs_recv.at[h, 27])
        total = total + zc[h].astype(F32) + zd[h].astype(F32)
        block = rows(block_at(y, z), BLOCK)
        dp[h, 0, block, :] = (total[0] * FACTOR).astype(BF16)
        dp[h, 1, block, :] = total[1].astype(BF16)
        give(h, 2, dp.at[h, :, partner_rows, :], pdqkv.at[1:3, :, lanes(core, h)])
        keep(h, 4, dp.at[h, :, own_rows, :], pdqkv.at[1:3, :, lanes(core, h)])

    def gradient_steps(h, events):
        def body(step, carry):
            gradients(h, (z + 10 - step - step // 2 + 2 * (step // 3)) % 4)
            for when, event in enumerate(events):
                pl.when(step == when)(event)
            return carry

        lax.fori_loop(0, 4, body, 0)

    def await_pair(s):
        await_bytes(held(s, seq * OWN, OWN), pair_recv.at[s])

    def await_rest():
        for copy in local:
            copy.wait()
        for slot in range(4, 8):
            await_bytes(x.at[0, 0, own_query, :], pair_recv.at[slot])
        await_bytes(v01.at[other], pair_recv.at[8])

    def first_scores(h):
        if h == 0:
            await_rest()
        await_pair(2 * h)
        await_swap(h, 0)
        scores(h, y)

    def side_scores(h):
        scores(h, y_right)
        scores(h, y_left)

    own_z(2)
    own_y(1)
    swap(1, 2, 0)
    own_z(0)
    for h in range(2):
        remote(
            pqkv.at[0, :, lanes(other, h)], x.at[h, 0, own_query, :],
            pair_send.at[4 + h], pair_recv.at[4 + h], partner,
        )
        remote(
            pgrad.at[:, lanes(other, h)], x.at[h, 3, own_query, :],
            pair_send.at[6 + h], pair_recv.at[6 + h], partner,
        )
    remote(v01.at[core], v01.at[core], pair_send.at[8], pair_recv.at[8], partner)
    tops[...] = jnp.full(tops.shape, MASKED, F32)
    own_y(0)
    swap(1, 1, 0)
    swap(0, 0, 0)
    own_y(2)
    own_y(3)
    own_z(1)
    y_forward(1, 0)
    swap(1, 2, 1)
    y_forward(0, 0)
    own_pair(2)
    z_forward(2)
    z_forward(0)
    z_forward(1)
    y_forward(3, 0)
    own_pair(3)
    own_z(3)
    z_end(2)
    swap(0, 0, 1)
    own_pair(0)
    z_end(0)
    swap(0, 1, 0)
    z_end(1)
    y_forward(0, 2)
    z_forward(3)
    swap(0, 2, 0)
    swap(0, 1, 1)
    swap(1, 0, 0)
    y_forward(0, 1)
    y_forward(0, 3)
    swap(0, 2, 1)
    y_forward(1, 2)
    y_forward(1, 1)
    y_forward(1, 3)
    own_pair(1)
    y_forward(2, 0)
    swap(1, 1, 1)
    y_forward(2, 2)
    y_forward(2, 1)
    y_forward(2, 3)
    first_scores(0)
    z_end(3)
    side_scores(0)
    y_forward(3, 2)
    y_forward(3, 1)
    swap(1, 0, 1)
    y_end(0)
    scores(0, y_far)
    exponentials(0)
    y_end(1)
    await_pair(1)
    outputs(0)

    def head_0_step_0():
        y_forward(3, 3)
        y_first(0, 0)
        y_end(2)

    def head_0_step_1():
        pass

    def head_0_step_2():
        y_second(0, 0)

    gradient_steps(0, (head_0_step_0, head_0_step_1, head_0_step_2))
    first_scores(1)
    y_first(0, 2)
    scores(1, y_far)
    side_scores(1)
    exponentials(1)
    y_end(3)
    y_third(0, 0)
    await_pair(3)
    outputs(1)

    def head_1_step_0():
        y_first(1, 0)
        y_first(0, 1)
        rest(0)
        y_second(1, 0)
        y_third(0, 2)

    def head_1_step_1():
        y_second(0, 1)
        z_first(0)
        y_first(1, 1)

    def head_1_step_2():
        y_third(1, 0)

    gradient_steps(1, (head_1_step_0, head_1_step_1, head_1_step_2))
    y_second(0, 2)
    y_first(1, 2)
    y_third(0, 1)
    rest(1)
    y_second(1, 2)
    y_first(0, 3)
    y_second(1, 1)
    y_first(1, 3)
    y_second(0, 3)
    z_first(1)
    y_third(1, 2)
    z_second(0, 1)
    y_third(1, 1)
    z_second(0, 2)
    y_third(0, 3)
    z_second(1, 2)
    z_second(1, 1)
    y_third(1, 3)
    y_second(1, 3)
    finish_queries(0)
    finish_queries(1)
    finish_keys(0)
    finish_keys(1)

    for s in range(4):
        for slot in range(24):
            size = BLOCK if slot >= 12 and slot % 4 < 2 else OWN
            await_bytes(held(s, 0, size), ag_send.at[s, slot])
    for slot in range(8):
        await_bytes(x.at[0, 0, own_query, :], pair_send.at[slot])
    await_bytes(v01.at[core], pair_send.at[8])
    sent = (PEERS - 1) * TOKENS
    for h in range(2):
        for slot in range(28):
            await_bytes(dp_rows(h, 0, OWN if slot < 26 else BLOCK), rs_send.at[h, slot])
        for group in range(3):
            for cross in range(2):
                await_bytes(swapped(h, group, cross), swap_send.at[h, cross, group])
        for group, ref in enumerate((y_buf.at[h, 3, 0:sent, :], y_buf.at[h, 0:3, 0:sent, :])):
            await_bytes(ref, back_send.at[h, group])
            await_bytes(ref, back_recv.at[h, group])
        theirs = lanes(other, h)
        arrivals = (pout.at[:, theirs], pdqkv.at[0, :, theirs], pdqkv.at[1:3, :, theirs])
        for slot, ref in enumerate(arrivals):
            await_bytes(ref, last_send.at[h, slot])
            await_bytes(ref, last_recv.at[h, slot])
    for copy in final:
        copy.wait()


def place(*refs):
    sources, targets, held, sem = refs[:4], refs[4:8], refs[8:12], refs[12]
    into = [pltpu.make_async_copy(sources[i], held[i], sem.at[0, i]) for i in range(4)]
    out = [pltpu.make_async_copy(held[i], targets[i], sem.at[1, i]) for i in range(4)]
    for copy in into:
        copy.start()
    for i in range(4):
        into[i].wait()
        out[i].start()
    for copy in out:
        copy.wait()


def local(prompt_qkv, prompt_grad, comp_qkv, comp_grad, lengths, keep_mask):
    hbm = pl.BlockSpec(memory_space=pl.ANY)
    vmem = pltpu.VMEM
    dma = pltpu.SemaphoreType.DMA
    results = pl.pallas_call(
        kernel,
        out_shape=(
            jax.ShapeDtypeStruct((OWN, 4 * HEAD_DIM), BF16),
            jax.ShapeDtypeStruct((1, TOKENS, 2 * PEERS * HEAD_DIM), BF16),
            jax.ShapeDtypeStruct((3, OWN, 4 * HEAD_DIM), BF16),
            jax.ShapeDtypeStruct((3, 1, TOKENS, 2 * PEERS * HEAD_DIM), BF16),
        ),
        in_specs=[
            hbm,
            hbm,
            hbm,
            hbm,
            pl.BlockSpec(memory_space=pltpu.SMEM),
            pl.BlockSpec(memory_space=pltpu.VMEM),
        ],
        out_specs=(hbm, hbm, hbm, hbm),
        scratch_shapes=[
            vmem((2, 2, PROMPT, HEAD_DIM), BF16),
            vmem((2, 4, ROWS, HEAD_DIM), BF16),
            vmem((2, SLOTS, HEAD_DIM), F32),
            vmem((2, PROMPT, ROWS), F32),
            vmem((2, PROMPT, ROWS), BF16),
            vmem((2, COMP_ROWS, SLOTS), F32),
            vmem((2, COMP_ROWS, SLOTS), BF16),
            vmem((2, PROMPT, ROWS), BF16),
            vmem((2, 8, ROWS), F32),
            vmem((2, HEAD_DIM, ROWS), F32),
            vmem((2, 8, ROWS), F32),
            vmem((2, ROWS, HEAD_DIM), BF16),
            vmem((2, 8, ROWS), F32),
            vmem((2, 2, PROMPT, HEAD_DIM), BF16),
            vmem((2, 4, ROWS, HEAD_DIM), BF16),
            vmem((2, 4, 2, OWN, HEAD_DIM), BF16),
            vmem((2, 4, 2, OWN, HEAD_DIM), BF16),
            vmem((2, 4, 2, BLOCK, HEAD_DIM), BF16),
            vmem((2, 4, 2, BLOCK, HEAD_DIM), BF16),
            vmem((2, 2, OWN, HEAD_DIM), BF16),
            vmem((2, 2, OWN, HEAD_DIM), BF16),
            vmem((2, 2, BLOCK, HEAD_DIM), BF16),
            vmem((2, 2, BLOCK, HEAD_DIM), BF16),
            dma((2, 5)),
            dma((2, 5)),
            dma((9,)),
            dma((9,)),
            dma((2, 2, 3)),
            dma((2, 2, 3)),
            dma((4, 24)),
            dma((4, 24)),
            dma((2, 28)),
            dma((2, 28)),
            dma((2, 2)),
            dma((2, 2)),
            dma((2, 3)),
            dma((2, 3)),
        ],
        compiler_params=pltpu.CompilerParams(
            collective_id=0, has_side_effects=True, vmem_limit_bytes=56 * 1024 * 1024
        ),
        name="attention",
    )(prompt_qkv, prompt_grad, comp_qkv, comp_grad, lengths, keep_mask)
    return pl.pallas_call(
        place,
        out_shape=tuple(jax.ShapeDtypeStruct(r.shape, r.dtype) for r in results),
        in_specs=[hbm] * 4,
        out_specs=(hbm,) * 4,
        scratch_shapes=[vmem(r.shape, r.dtype) for r in results] + [dma((2, 4))],
        compiler_params=pltpu.CompilerParams(vmem_limit_bytes=56 * 1024 * 1024),
        name="place",
    )(*results)


def solution(mesh):
    in_specs = (
        P(None, "seq", "head"),
        P("seq", "head"),
        P(None, "seq", "head", None),
        P("seq", "head", None),
        P("seq"),
        P("seq", None),
    )
    out_specs = (
        P("seq", "head"),
        P("seq", "head", None),
        P(None, "seq", "head"),
        P(None, "seq", "head", None),
    )
    return jax.shard_map(local, mesh=mesh, in_specs=in_specs, out_specs=out_specs, check_vma=False)
```

time: 277 us -> 69.7 us (0.25)
  local copies, waits for them, and re-layouts: 94.8 us -> 0 us
  Pallas kernels: 0 us -> 67.7 us
  waiting for transfers between devices: 66 us -> 0 us
  matrix products: 38.9 us -> 0 us
  other arithmetic: 38.3 us -> 0 us
  starting transfers between devices: 20.6 us -> 0 us
  between operations: 15.1 us -> 1.29 us
    pallas_call x0 -> x2, Pallas kernels: none -> 67.7 us  [the longest x1 65.4 us: local(): pl.pallas_call(kernel, out_shape=(jax.ShapeDtypeStruct((OWN, 4 * HEAD_DIM...]
    unnamed x42 -> x0, local copies, waits for them, and re-layouts: 49.4 us -> none
    reduce_scatter x1 -> x0, waiting for transfers between devices: 44.4 us -> none  [local(): lax.psum_scatter(jnp.concatenate([dkeys.reshape(count, -1), dvalues.resha...]
    dot_general x18 -> x0, matrix products: 38.9 us -> none  [the longest x1 7.81 us: local(): jnp.einsum('chlp,clhe->phe', weight_far, comp_cot, preferred_element_type...]
    unnamed x2 -> x0, other arithmetic: 26.3 us -> none
    all_to_all x4 -> x0, waiting for transfers between devices: 21.6 us -> none  [the longest x1 11.3 us: local(): lax.all_to_all(comp_qkv, 'head', split_axis=3, concat_axis=2, tiled=True)]
    all_to_all x4 -> x0, starting transfers between devices: 20.4 us -> none  [the longest x1 6.2 us: local(): lax.all_to_all(comp_grad[None], 'head', split_axis=3, concat_axis=2, tile...]
    slice x8 -> x0, local copies, waits for them, and re-layouts: 11.2 us -> none  [the longest x1 9.98 us: local(): prompt_keys = gathered[0].reshape(-1, local_heads, HEAD_DIM)]
  transfers between devices with their start and end apart: 6 -> 0, of which waited for: 3 -> 0; matrix products, arithmetic and copies ran while one was open for 34% -> 0% of each run, Pallas kernels for 0% -> 0%
where the time goes in v4:
time: 69.7 us; the launch traced here: 69 us
  Pallas kernels  67.7 us (97%)
  between operations  1.29 us (2%)
    pallas_call x1, Pallas kernels, local(): pl.pallas_call(kernel, out_shape=(jax.ShapeDtypeStruct((OWN, 4 * HEAD_DIM...  65.4 us
    pallas_call x1, Pallas kernels, local(): pl.pallas_call(place, out_shape=tuple((jax.ShapeDtypeStruct(r.shape, r.dt...  2.29 us

profile of v4, /device:TPU:1, one launch (start us, length us, event | category | flops | bytes accessed | tf_op | source)
XLA Modules:
  0.0 69.0 jit_solution(11723202353339859856)
XLA Ops:
  1.3 65.4 %attention.1 = (bf16[64,512]{1,0:T(8,128)(2,1)}, bf16[1,32,4096]{2,1,0:T(8,128)(2,1)}, bf16[3,64,512]{2,1,0:T(8,128)(2,1)}, bf16[3,1,32,4096]{3,2,1,0:T(8,128)(2,1)}) custom-call(bf16[3,64,512]{2,1,0:T(8,128)(2,1)} %pqkv.1, bf16[64,512]{1,0:T(8,128)(2,1)} %pgrad.1, bf16[3,1,32,4096]{3,2,1,0:T(8,128)(2,1)} %cqkv.1, bf16[1,32,4096]{2,1,0:T(8,128)(2,1)} %cgrad.1, ...), custom_call_target="tpu_custom_call" | custom-call | tf_op jit(solution)/shard_map/attention/pallas_call | solution.py:626
  66.7 2.3 %place.1 = (bf16[64,512]{1,0:T(8,128)(2,1)}, bf16[1,32,4096]{2,1,0:T(8,128)(2,1)}, bf16[3,64,512]{2,1,0:T(8,128)(2,1)}, bf16[3,1,32,4096]{3,2,1,0:T(8,128)(2,1)}) custom-call(bf16[64,512]{1,0:T(8,128)(2,1)} %get-tuple-element.8.refs_0_, bf16[1,32,4096]{2,1,0:T(8,128)(2,1)} %get-tuple-element.9.refs_1_, bf16[3,64,512]{2,1,0:T(8,128)(2,1)} %get-tuple-element.10.refs_2_, ...), custom_call_target="tpu_custom_call" | custom-call | tf_op jit(solution)/shard_map/place/pallas_call | solution.py:687

commit v5 on v4

--- a/solution.py
+++ b/solution.py
@@ -451,10 +451,10 @@
         scores(h, y_right)
         scores(h, y_left)
 
-    own_z(2)
+    own_z(0)
+    own_y(0)
+    swap(0, 0, 0)
     own_y(1)
-    swap(1, 2, 0)
-    own_z(0)
     for h in range(2):
         remote(
             pqkv.at[0, :, lanes(other, h)], x.at[h, 0, own_query, :],
@@ -466,115 +466,116 @@
         )
     remote(v01.at[core], v01.at[core], pair_send.at[8], pair_recv.at[8], partner)
     tops[...] = jnp.full(tops.shape, MASKED, F32)
-    own_y(0)
-    swap(1, 1, 0)
-    swap(0, 0, 0)
+    swap(0, 2, 0)
+    own_z(1)
+    own_pair(3)
+    own_pair(1)
     own_y(2)
+    own_z(3)
     own_y(3)
-    own_z(1)
+    z_forward(0)
+    y_forward(0, 0)
+    own_z(2)
     y_forward(1, 0)
-    swap(1, 2, 1)
-    y_forward(0, 0)
-    own_pair(2)
-    z_forward(2)
-    z_forward(0)
     z_forward(1)
-    y_forward(3, 0)
-    own_pair(3)
-    own_z(3)
-    z_end(2)
     swap(0, 0, 1)
-    own_pair(0)
+    z_forward(3)
     z_end(0)
     swap(0, 1, 0)
+    y_forward(0, 2)
     z_end(1)
-    y_forward(0, 2)
-    z_forward(3)
-    swap(0, 2, 0)
-    swap(0, 1, 1)
+    own_pair(0)
+    swap(1, 1, 0)
+    z_forward(2)
     swap(1, 0, 0)
+    own_pair(2)
+    swap(0, 2, 1)
     y_forward(0, 1)
+    swap(1, 2, 1)
     y_forward(0, 3)
-    swap(0, 2, 1)
+    swap(1, 2, 0)
+    y_forward(3, 2)
     y_forward(1, 2)
     y_forward(1, 1)
+    swap(0, 1, 1)
+    z_end(3)
     y_forward(1, 3)
-    own_pair(1)
-    y_forward(2, 0)
-    swap(1, 1, 1)
+    first_scores(0)
+    side_scores(0)
+    z_end(2)
+    swap(1, 0, 1)
     y_forward(2, 2)
-    y_forward(2, 1)
-    y_forward(2, 3)
-    first_scores(0)
-    z_end(3)
-    side_scores(0)
-    y_forward(3, 2)
     y_forward(3, 1)
-    swap(1, 0, 1)
     y_end(0)
     scores(0, y_far)
     exponentials(0)
+    y_forward(2, 1)
+    swap(1, 1, 1)
+    y_forward(3, 0)
+    y_forward(3, 3)
+    y_forward(2, 0)
     y_end(1)
     await_pair(1)
     outputs(0)
+    y_forward(2, 3)
 
     def head_0_step_0():
-        y_forward(3, 3)
+        pass
+
+    def head_0_step_1():
         y_first(0, 0)
-        y_end(2)
-
-    def head_0_step_1():
+
+    def head_0_step_2():
         pass
-
-    def head_0_step_2():
-        y_second(0, 0)
 
     gradient_steps(0, (head_0_step_0, head_0_step_1, head_0_step_2))
     first_scores(1)
+    y_second(0, 2)
+    side_scores(1)
+    y_end(3)
+    y_first(0, 1)
+    y_second(0, 0)
     y_first(0, 2)
+    y_second(0, 1)
+    y_end(2)
     scores(1, y_far)
-    side_scores(1)
     exponentials(1)
-    y_end(3)
-    y_third(0, 0)
     await_pair(3)
     outputs(1)
+    y_third(0, 0)
 
     def head_1_step_0():
         y_first(1, 0)
-        y_first(0, 1)
         rest(0)
         y_second(1, 0)
         y_third(0, 2)
 
     def head_1_step_1():
-        y_second(0, 1)
+        y_first(1, 1)
+
+    def head_1_step_2():
+        y_first(1, 2)
         z_first(0)
-        y_first(1, 1)
-
-    def head_1_step_2():
         y_third(1, 0)
 
     gradient_steps(1, (head_1_step_0, head_1_step_1, head_1_step_2))
-    y_second(0, 2)
-    y_first(1, 2)
     y_third(0, 1)
-    rest(1)
+    y_third(1, 1)
     y_second(1, 2)
-    y_first(0, 3)
+    z_first(1)
     y_second(1, 1)
-    y_first(1, 3)
-    y_second(0, 3)
-    z_first(1)
     y_third(1, 2)
     z_second(0, 1)
-    y_third(1, 1)
+    y_first(1, 3)
     z_second(0, 2)
+    y_first(0, 3)
+    z_second(1, 1)
+    y_second(0, 3)
+    z_second(1, 2)
+    y_second(1, 3)
+    y_third(1, 3)
     y_third(0, 3)
-    z_second(1, 2)
-    z_second(1, 1)
-    y_third(1, 3)
-    y_second(1, 3)
+    rest(1)
     finish_queries(0)
     finish_queries(1)
     finish_keys(0)
@@ -607,15 +608,11 @@
 
 
 def place(*refs):
-    sources, targets, held, sem = refs[:4], refs[4:8], refs[8:12], refs[12]
-    into = [pltpu.make_async_copy(sources[i], held[i], sem.at[0, i]) for i in range(4)]
-    out = [pltpu.make_async_copy(held[i], targets[i], sem.at[1, i]) for i in range(4)]
-    for copy in into:
+    sources, targets, sem = refs[:4], refs[4:8], refs[8]
+    copies = [pltpu.make_async_copy(sources[i], targets[i], sem.at[i]) for i in range(4)]
+    for copy in copies:
         copy.start()
-    for i in range(4):
-        into[i].wait()
-        out[i].start()
-    for copy in out:
+    for copy in copies:
         copy.wait()
 
 
@@ -626,10 +623,10 @@
     results = pl.pallas_call(
         kernel,
         out_shape=(
-            jax.ShapeDtypeStruct((OWN, 4 * HEAD_DIM), BF16),
-            jax.ShapeDtypeStruct((1, TOKENS, 2 * PEERS * HEAD_DIM), BF16),
-            jax.ShapeDtypeStruct((3, OWN, 4 * HEAD_DIM), BF16),
-            jax.ShapeDtypeStruct((3, 1, TOKENS, 2 * PEERS * HEAD_DIM), BF16),
+            vmem((OWN, 4 * HEAD_DIM), BF16),
+            vmem((1, TOKENS, 2 * PEERS * HEAD_DIM), BF16),
+            vmem((3, OWN, 4 * HEAD_DIM), BF16),
+            vmem((3, 1, TOKENS, 2 * PEERS * HEAD_DIM), BF16),
         ),
         in_specs=[
             hbm,
@@ -639,7 +636,7 @@
             pl.BlockSpec(memory_space=pltpu.SMEM),
             pl.BlockSpec(memory_space=pltpu.VMEM),
         ],
-        out_specs=(hbm, hbm, hbm, hbm),
+        out_specs=(pl.BlockSpec(memory_space=vmem),) * 4,
         scratch_shapes=[
             vmem((2, 2, PROMPT, HEAD_DIM), BF16),
             vmem((2, 4, ROWS, HEAD_DIM), BF16),
@@ -687,12 +684,11 @@
     return pl.pallas_call(
         place,
         out_shape=tuple(jax.ShapeDtypeStruct(r.shape, r.dtype) for r in results),
-        in_specs=[hbm] * 4,
+        in_specs=[pl.BlockSpec(memory_space=vmem)] * 4,
         out_specs=(hbm,) * 4,
-        scratch_shapes=[vmem(r.shape, r.dtype) for r in results] + [dma((2, 4))],
-        compiler_params=pltpu.CompilerParams(vmem_limit_bytes=56 * 1024 * 1024),
+        scratch_shapes=[dma((4,))],
         name="place",
-    )(*results)
+    )(*[pltpu.with_memory_space_constraint(r, vmem) for r in results])
 
 
 def solution(mesh):

time: 69.7 us -> 66.4 us (0.953)
  Pallas kernels: 67.7 us -> 65.1 us
    pallas_call x1, Pallas kernels: 65.4 us -> 64 us  [local(): pl.pallas_call(kernel, out_shape=(vmem((OWN, 4 * HEAD_DIM), BF16), vmem((...]
    pallas_call x1, Pallas kernels: 2.29 us -> 1.09 us  [local(): pl.pallas_call(place, out_shape=tuple((jax.ShapeDtypeStruct(r.shape, r.dt...]
where the time goes in v5:
time: 66.4 us; the launch traced here: 66.3 us
  Pallas kernels  65.1 us (98%)
  between operations  1.29 us (2%)
    pallas_call x1, Pallas kernels, local(): pl.pallas_call(kernel, out_shape=(vmem((OWN, 4 * HEAD_DIM), BF16), vmem((...  64 us

profile of v5, /device:TPU:1, one launch (start us, length us, event | category | flops | bytes accessed | tf_op | source)
XLA Modules:
  0.0 66.3 jit_solution(9118746911224079212)
XLA Ops:
  1.3 64.0 %attention.1 = (bf16[64,512]{1,0:T(8,128)(2,1)S(1)}, bf16[1,32,4096]{2,1,0:T(8,128)(2,1)S(1)}, bf16[3,64,512]{2,1,0:T(8,128)(2,1)S(1)}, bf16[3,1,32,4096]{3,2,1,0:T(8,128)(2,1)S(1)}) custom-call(bf16[3,64,512]{2,1,0:T(8,128)(2,1)} %pqkv.1, bf16[64,512]{1,0:T(8,128)(2,1)} %pgrad.1, bf16[3,1,32,4096]{3,2,1,0:T(8,128)(2,1)} %cqkv.1, ...), custom_call_target="tpu_custom_call" | custom-call | tf_op jit(solution)/shard_map/attention/pallas_call | solution.py:623
  65.3 1.1 %place.1 = (bf16[64,512]{1,0:T(8,128)(2,1)}, bf16[1,32,4096]{2,1,0:T(8,128)(2,1)}, bf16[3,64,512]{2,1,0:T(8,128)(2,1)}, bf16[3,1,32,4096]{3,2,1,0:T(8,128)(2,1)}) custom-call(bf16[64,512]{1,0:T(8,128)(2,1)S(1)} %get-tuple-element.8.refs_0_, bf16[1,32,4096]{2,1,0:T(8,128)(2,1)S(1)} %get-tuple-element.9.refs_1_, ...), custom_call_target="tpu_custom_call" | custom-call | tf_op jit(solution)/shard_map/place/pallas_call | solution.py:684

commit v6 on v5

--- a/solution.py
+++ b/solution.py
@@ -466,115 +466,113 @@
         )
     remote(v01.at[core], v01.at[core], pair_send.at[8], pair_recv.at[8], partner)
     tops[...] = jnp.full(tops.shape, MASKED, F32)
-    swap(0, 2, 0)
     own_z(1)
-    own_pair(3)
+    own_y(3)
+    own_y(2)
+    swap(1, 0, 0)
+    own_z(2)
     own_pair(1)
-    own_y(2)
+    own_pair(2)
+    own_pair(0)
+    y_forward(0, 0)
     own_z(3)
-    own_y(3)
     z_forward(0)
-    y_forward(0, 0)
-    own_z(2)
+    y_forward(3, 0)
     y_forward(1, 0)
     z_forward(1)
+    z_forward(2)
     swap(0, 0, 1)
+    z_end(0)
+    z_end(1)
+    swap(1, 1, 0)
+    swap(1, 2, 0)
+    y_forward(0, 1)
+    swap(0, 2, 0)
+    z_end(2)
+    own_pair(3)
     z_forward(3)
-    z_end(0)
     swap(0, 1, 0)
+    swap(0, 2, 1)
+    swap(0, 1, 1)
     y_forward(0, 2)
-    z_end(1)
-    own_pair(0)
-    swap(1, 1, 0)
-    z_forward(2)
-    swap(1, 0, 0)
-    own_pair(2)
-    swap(0, 2, 1)
-    y_forward(0, 1)
+    y_forward(0, 3)
+    swap(1, 0, 1)
+    y_forward(1, 1)
+    y_forward(1, 3)
+    y_forward(1, 2)
     swap(1, 2, 1)
-    y_forward(0, 3)
-    swap(1, 2, 0)
-    y_forward(3, 2)
-    y_forward(1, 2)
-    y_forward(1, 1)
-    swap(0, 1, 1)
+    swap(1, 1, 1)
+    y_forward(2, 0)
     z_end(3)
-    y_forward(1, 3)
     first_scores(0)
     side_scores(0)
-    z_end(2)
-    swap(1, 0, 1)
+    y_forward(3, 1)
+    y_forward(3, 2)
+    y_forward(2, 1)
+    y_forward(2, 3)
     y_forward(2, 2)
-    y_forward(3, 1)
     y_end(0)
     scores(0, y_far)
     exponentials(0)
-    y_forward(2, 1)
-    swap(1, 1, 1)
-    y_forward(3, 0)
-    y_forward(3, 3)
-    y_forward(2, 0)
     y_end(1)
     await_pair(1)
     outputs(0)
-    y_forward(2, 3)
 
     def head_0_step_0():
-        pass
+        y_first(0, 0)
+        y_forward(3, 3)
 
     def head_0_step_1():
-        y_first(0, 0)
+        y_first(0, 1)
 
     def head_0_step_2():
-        pass
+        y_first(0, 2)
 
     gradient_steps(0, (head_0_step_0, head_0_step_1, head_0_step_2))
+    y_end(2)
     first_scores(1)
+    scores(1, y_far)
+    y_second(0, 0)
+    side_scores(1)
+    exponentials(1)
+    y_end(3)
     y_second(0, 2)
-    side_scores(1)
-    y_end(3)
-    y_first(0, 1)
-    y_second(0, 0)
-    y_first(0, 2)
+    y_third(0, 0)
     y_second(0, 1)
-    y_end(2)
-    scores(1, y_far)
-    exponentials(1)
     await_pair(3)
     outputs(1)
-    y_third(0, 0)
+    y_third(0, 2)
 
     def head_1_step_0():
         y_first(1, 0)
         rest(0)
         y_second(1, 0)
-        y_third(0, 2)
 
     def head_1_step_1():
         y_first(1, 1)
 
     def head_1_step_2():
         y_first(1, 2)
+        y_third(1, 0)
         z_first(0)
-        y_third(1, 0)
 
     gradient_steps(1, (head_1_step_0, head_1_step_1, head_1_step_2))
     y_third(0, 1)
     y_third(1, 1)
+    y_second(1, 1)
+    y_first(0, 3)
+    z_first(1)
     y_second(1, 2)
-    z_first(1)
-    y_second(1, 1)
     y_third(1, 2)
+    z_second(0, 2)
     z_second(0, 1)
     y_first(1, 3)
-    z_second(0, 2)
-    y_first(0, 3)
+    y_third(0, 3)
+    y_second(1, 3)
     z_second(1, 1)
+    z_second(1, 2)
     y_second(0, 3)
-    z_second(1, 2)
-    y_second(1, 3)
     y_third(1, 3)
-    y_third(0, 3)
     rest(1)
     finish_queries(0)
     finish_queries(1)

time: 66.4 us -> 65.2 us (0.982)
  Pallas kernels: 65.1 us -> 63.8 us
    pallas_call x1, Pallas kernels: 64 us -> 62.7 us  [local(): pl.pallas_call(kernel, out_shape=(vmem((OWN, 4 * HEAD_DIM), BF16), vmem((...]
where the time goes in v6:
time: 65.2 us; the launch traced here: 65.1 us
  Pallas kernels  63.8 us (98%)
  between operations  1.29 us (2%)
    pallas_call x1, Pallas kernels, local(): pl.pallas_call(kernel, out_shape=(vmem((OWN, 4 * HEAD_DIM), BF16), vmem((...  62.7 us

profile of v6, /device:TPU:1, one launch (start us, length us, event | category | flops | bytes accessed | tf_op | source)
XLA Modules:
  0.0 65.1 jit_solution(17505250901675704319)
XLA Ops:
  1.3 62.7 %attention.1 = (bf16[64,512]{1,0:T(8,128)(2,1)S(1)}, bf16[1,32,4096]{2,1,0:T(8,128)(2,1)S(1)}, bf16[3,64,512]{2,1,0:T(8,128)(2,1)S(1)}, bf16[3,1,32,4096]{3,2,1,0:T(8,128)(2,1)S(1)}) custom-call(bf16[3,64,512]{2,1,0:T(8,128)(2,1)} %pqkv.1, bf16[64,512]{1,0:T(8,128)(2,1)} %pgrad.1, bf16[3,1,32,4096]{3,2,1,0:T(8,128)(2,1)} %cqkv.1, ...), custom_call_target="tpu_custom_call" | custom-call | tf_op jit(solution)/shard_map/attention/pallas_call | solution.py:621
  64.0 1.1 %place.1 = (bf16[64,512]{1,0:T(8,128)(2,1)}, bf16[1,32,4096]{2,1,0:T(8,128)(2,1)}, bf16[3,64,512]{2,1,0:T(8,128)(2,1)}, bf16[3,1,32,4096]{3,2,1,0:T(8,128)(2,1)}) custom-call(bf16[64,512]{1,0:T(8,128)(2,1)S(1)} %get-tuple-element.8.refs_0_, bf16[1,32,4096]{2,1,0:T(8,128)(2,1)S(1)} %get-tuple-element.9.refs_1_, ...), custom_call_target="tpu_custom_call" | custom-call | tf_op jit(solution)/shard_map/place/pallas_call | solution.py:682
